TPU v7x, 32 devices: a whole 2x2x4 slice. The times are simulated.
32 devices in a mesh: dp: 8 (over z, y), mp: 4 (over x, core).
Axes of the slice: x: 2, y: 2, z: 4, core: 2. Of those that a mesh axis runs over, the one named last changes fastest.
Arguments:
- texts: bfloat16 [128, 35, 768], P('dp'), may hold values from -6 to 6
- query_weight: bfloat16 [768, 768], P('mp'), may hold values from -0.21875 to 0.21875
- patch_key_value: bfloat16 [32, 12, 577, 128], P('dp', 'mp'), may hold values from -300 to 300
- grad_out: bfloat16 [128, 4, 35, 768], P('dp'), may hold values from -6 to 6
- negatives: int32 [128, 3], P('dp'), may hold values from 0 to 31, as said below
Outputs:
- text_grad: bfloat16 [128, 35, 768], P(('dp', 'mp'))
- weight_grad: float32 [768, 768], P('mp')
- key_value_grad: bfloat16 [32, 12, 577, 128], P('dp', 'mp')
Inputs may be any that keep to these rules, and one draw needn't show every extreme that they name: Never an image whose index // 4 equals the text's index // 16. Among the negatives of the texts of one index of dp, at most 12 name images of any one index; some pair of indices reaches 12.
All inputs are finite; a program needn't handle non-finite values.
Results may differ from a plain program's by a relative error of at most 0.03.
The roundings to bfloat16 on the way count: a program that leaves them out, or rounds other values in their place, can miss the bound.
Values may be sent and summed in bfloat16 or wider, within the bound.
A program may use at most 192 MiB of HBM per device.

v0:
```python
import math

import jax
import jax.numpy as jnp
from jax import lax
from jax.sharding import PartitionSpec as P

HEAD_SIZE = 64
NEG = 3


def pair_grads(query, cotangent, memory):
    scale = HEAD_SIZE ** (-0.5)
    q4 = query.reshape(query.shape[:-1] + (-1, HEAD_SIZE))
    g4 = cotangent.reshape(cotangent.shape[:-1] + (-1, HEAD_SIZE))
    k4 = memory[..., :HEAD_SIZE]
    v4 = memory[..., HEAD_SIZE:]
    scores = jnp.einsum("blhd,bhkd->bhlk", q4, k4, preferred_element_type=jnp.float32) * scale
    probs_f = jax.nn.softmax(scores, axis=-1)
    probs = probs_f.astype(jnp.bfloat16)
    dprobs = jnp.einsum("blhd,bhkd->bhlk", g4, v4, preferred_element_type=jnp.float32)
    center = jnp.sum(probs_f * dprobs, axis=-1, keepdims=True)
    dscores = (probs_f * (dprobs - center) * scale).astype(jnp.bfloat16)
    pair_dv = jnp.einsum("bhlk,blhd->bhkd", probs, g4, preferred_element_type=jnp.float32)
    pair_dq = jnp.einsum("bhlk,bhkd->blhd", dscores, k4, preferred_element_type=jnp.float32)
    pair_dk = jnp.einsum("bhlk,blhd->bhkd", dscores, q4, preferred_element_type=jnp.float32)
    pair_dq = pair_dq.reshape(pair_dq.shape[:2] + (-1,))
    return (pair_dq, jnp.concatenate([pair_dk, pair_dv], axis=-1))


def serve(query_rows, grad_rows, image_ids, patch_key_value):
    count, length, width = query_rows.shape
    size = math.gcd(count, 16)
    steps = count // size

    def visit(memory_acc, item):
        query_tile, g_block, ids = item
        memory = jnp.take(patch_key_value, ids, axis=0)
        pair_dq, pair_dkv = pair_grads(query_tile, g_block, memory)
        memory_acc = memory_acc.at[ids].add(pair_dkv)
        return (memory_acc, pair_dq)

    start = jnp.zeros(patch_key_value.shape, jnp.float32)
    items = (
        query_rows.reshape(steps, size, length, width),
        grad_rows.reshape(steps, size, length, width),
        image_ids.reshape(steps, size),
    )
    memory_acc, dquery = lax.scan(visit, start, items)
    return (dquery.reshape(count, length, width), memory_acc)


def per_device(texts, query_weight, patch_key_value, grad_out, negatives):
    owning_devices = lax.axis_size("dp")
    texts_here, length, _ = texts.shape
    local_images = patch_key_value.shape[0]
    captions = texts_here // local_images
    wanted = NEG * texts_here
    capacity = 2 * max(1, wanted // owning_devices)
    slots_all = owning_devices * capacity
    width = query_weight.shape[0]
    flat_text = texts.reshape(texts_here * length, -1)
    query = lax.dot_general(
        flat_text, query_weight, (((1,), (1,)), ((), ())), preferred_element_type=jnp.float32
    )
    query = query.astype(jnp.bfloat16).reshape(texts_here, length, width)
    grad_cols = lax.dynamic_slice_in_dim(grad_out, lax.axis_index("mp") * width, width, 3)
    flat_neg = negatives.reshape(-1)
    owner = flat_neg // local_images
    local_id = flat_neg % local_images
    owner_hot = (owner[:, None] == jnp.arange(owning_devices, dtype=jnp.int32)[None, :]).astype(
        jnp.int32
    )
    earlier = jnp.cumsum(owner_hot, axis=0) - owner_hot
    rank = jnp.sum(earlier * owner_hot, axis=1)
    slot = owner * capacity + rank
    placed = slot[None, :] == jnp.arange(slots_all, dtype=jnp.int32)[:, None]
    place = placed.astype(jnp.bfloat16)
    place_text = jnp.sum(placed.reshape(slots_all, texts_here, NEG), axis=2).astype(jnp.bfloat16)
    send_query = jnp.dot(
        place_text, query.reshape(texts_here, -1), preferred_element_type=jnp.float32
    )
    send_query = send_query.astype(jnp.bfloat16).reshape(owning_devices, capacity, length, width)
    send_grad = jnp.dot(
        place, grad_cols[:, 1:].reshape(wanted, -1), preferred_element_type=jnp.float32
    )
    send_grad = send_grad.astype(jnp.bfloat16).reshape(owning_devices, capacity, length, width)
    send_pair = jnp.concatenate([send_query, send_grad], axis=3)
    send_id = jnp.sum(jnp.where(placed, local_id[None, :], 0), axis=1)
    send_id = send_id.astype(jnp.bfloat16).reshape(owning_devices, capacity)
    own_ids = jnp.arange(texts_here, dtype=jnp.int32) // captions
    own_dq, own_dkv = serve(query, grad_cols[:, 0], own_ids, patch_key_value)
    got_pair, got_id = (
        lax.all_to_all(send_pair, "dp", split_axis=0, concat_axis=0, tiled=True),
        lax.all_to_all(send_id, "dp", split_axis=0, concat_axis=0, tiled=True),
    )
    remote_query_grad, far_dkv = serve(
        got_pair[..., :width].reshape(-1, length, width),
        got_pair[..., width:].reshape(-1, length, width),
        got_id.reshape(-1).astype(jnp.int32),
        patch_key_value,
    )
    returned = lax.all_to_all(
        remote_query_grad.reshape(owning_devices, capacity, length, width),
        "dp",
        split_axis=0,
        concat_axis=0,
        tiled=True,
    )
    returned = returned.reshape(slots_all, length, width)
    per_request = jnp.take(returned, slot, axis=0).reshape(texts_here, NEG, length, width)
    dquery = (own_dq + jnp.sum(per_request, axis=1)).astype(jnp.bfloat16)
    flat_dq = dquery.reshape(texts_here * length, width)
    weight_local = lax.dot_general(
        flat_dq, flat_text, (((0,), (0,)), ((), ())), preferred_element_type=jnp.float32
    )
    weight_grad = lax.psum(weight_local, "dp")
    text_term = jnp.dot(flat_dq, query_weight, preferred_element_type=jnp.float32)
    text_grad = lax.psum_scatter(
        text_term.reshape(texts_here, length, -1), "mp", scatter_dimension=0, tiled=True
    )
    key_value_grad = (own_dkv + far_dkv).astype(jnp.bfloat16)
    return (text_grad.astype(jnp.bfloat16), weight_grad, key_value_grad)


def solution(mesh):
    in_specs = (
        P("dp", None, None),
        P("mp", None),
        P("dp", "mp", None, None),
        P("dp", None, None, None),
        P("dp", None),
    )
    out_specs = (P(("dp", "mp"), None, None), P("mp", None), P("dp", "mp", None, None))
    return jax.shard_map(
        per_device, mesh=mesh, in_specs=in_specs, out_specs=out_specs, check_vma=False
    )
```

profile of v0, /device:TPU:0, one launch (start us, length us, event | category | flops | bytes accessed | tf_op | source)
XLA Modules:
  0.0 1215.0 jit_solution(12209435009536691090)
XLA Ops:
  10.2 7.3 all-to-all-start
  62.0 63.0 %all-to-all-done.1 = bf16[8,12,35,384]{3,2,1,0:T(8,128)(2,1)} async-done(((bf16[8,12,35,384]{3,2,1,0:T(8,128)(2,1)}), bf16[8,12,35,384]{3,2,1,0:T(8,128)(2,1)}, u32[]{:S(2)}, u32[]{:S(2)}) %all-to-all-start.1) | async-done | bytes 2580512 | tf_op jit(solution)/shard_map/all_to_all | solution.py:94
  133.2 861.7 %while.2 = (s32[]{:T(128)}, f32[4,3,577,128]{3,2,1,0:T(8,128)}, f32[6,16,35,192]{3,1,2,0:T(8,128)}, s32[6,16]{1,0:T(8,128)S(1)}, bf16[6,16,35,192]{3,1,2,0:T(8,1...) while((s32[]{:T(128)}, f32[4,3,577,128]{3,2,1,0:T(8,128)}, ...), condition=%wide.region_12.14_spmd, body=%wide.region_7.13_spmd.sunk | while | flops 650419136 | bytes 279351616 | solution.py:49
  145.7 10.2 copy.186
  155.8 7.3 broadcast_select_fusion.3
  172.9 19.7 %fusion.128 = f32[16,35,3,64]{3,1,2,0:T(8,128)} fusion(f32[16,3,35,577]{3,2,1,0:T(8,128)} %fusion.126, bf16[16,3,577,128]{2,3,1,0:T(8,128)(2,1)} %broadcast_select_fusion.3, f32[16,3,35,577]{3,2,1,0:T(8,128)} %get-tuple-element.189, f32[16,3,35]{2,1,0:T(4,128)S(1)} %get-tuple-element.190), kind=kOutput, calls=%fused_computation.26.clone.1 | convolution fusion | flops 130865856 | bytes 24088576 | tf_op jit(solution)/shard_map/while/body/eval_jaxpr/bhlk,bhkd->blhd/dot_general | solution.py:25
  197.5 20.3 %fusion.127 = f32[16,3,577,64]{2,3,1,0:T(8,128)} fusion(f32[16,3,35,577]{3,2,1,0:T(8,128)} %fusion.126, bf16[16,35,3,64]{3,2,0,1:T(4,128)(2,1)} %reshape.419, f32[16,3,35,577]{3,2,1,0:T(8,128)} %get-tuple-element.189, f32[16,3,35]{2,1,0:T(4,128)S(1)} %get-tuple-element.190), kind=kOutput, calls=%fused_computation.25.clone.1 | convolution fusion | flops 130865856 | bytes 15066816 | tf_op jit(solution)/shard_map/while/body/eval_jaxpr/bhlk,blhd->bhkd/dot_general | solution.py:26
  228.4 15.2 %copy.187 = f32[16,3,577,128]{3,2,1,0:T(8,128)} copy(f32[16,3,577,128]{2,3,1,0:T(8,128)} %pad_maximum_fusion.4) | data formatting | bytes 28360704 | tf_op jit(solution)/shard_map/while/body/eval_jaxpr/concatenate | solution.py:28
  243.6 29.0 %scatter_fusion = f32[4,3,577,128]{3,2,1,0:T(8,128)} fusion(f32[4,3,577,128]{3,2,1,0:T(8,128)} %get-tuple-element.200, s32[16]{0:T(128)S(1)} %fusion.122, f32[16,3,577,128]{3,2,1,0:T(8,128)} %copy.187), kind=kCustom, calls=%fused_computation.3.clone.1 | custom fusion | flops 3545088 | bytes 42541120 | tf_op jit(solution)/shard_map/while/body/eval_jaxpr/scatter-add | solution.py:40
  286.7 10.2 copy.186
  296.9 7.3 broadcast_select_fusion.3
  313.9 19.7 %fusion.128 = f32[16,35,3,64]{3,1,2,0:T(8,128)} fusion(f32[16,3,35,577]{3,2,1,0:T(8,128)} %fusion.126, bf16[16,3,577,128]{2,3,1,0:T(8,128)(2,1)} %broadcast_select_fusion.3, f32[16,3,35,577]{3,2,1,0:T(8,128)} %get-tuple-element.189, f32[16,3,35]{2,1,0:T(4,128)S(1)} %get-tuple-element.190), kind=kOutput, calls=%fused_computation.26.clone.1 | convolution fusion | flops 130865856 | bytes 24088576 | tf_op jit(solution)/shard_map/while/body/eval_jaxpr/bhlk,bhkd->blhd/dot_general | solution.py:25
  338.5 20.3 %fusion.127 = f32[16,3,577,64]{2,3,1,0:T(8,128)} fusion(f32[16,3,35,577]{3,2,1,0:T(8,128)} %fusion.126, bf16[16,35,3,64]{3,2,0,1:T(4,128)(2,1)} %reshape.419, f32[16,3,35,577]{3,2,1,0:T(8,128)} %get-tuple-element.189, f32[16,3,35]{2,1,0:T(4,128)S(1)} %get-tuple-element.190), kind=kOutput, calls=%fused_computation.25.clone.1 | convolution fusion | flops 130865856 | bytes 15066816 | tf_op jit(solution)/shard_map/while/body/eval_jaxpr/bhlk,blhd->bhkd/dot_general | solution.py:26
  369.4 15.2 %copy.187 = f32[16,3,577,128]{3,2,1,0:T(8,128)} copy(f32[16,3,577,128]{2,3,1,0:T(8,128)} %pad_maximum_fusion.4) | data formatting | bytes 28360704 | tf_op jit(solution)/shard_map/while/body/eval_jaxpr/concatenate | solution.py:28
  384.6 29.3 %scatter_fusion = f32[4,3,577,128]{3,2,1,0:T(8,128)} fusion(f32[4,3,577,128]{3,2,1,0:T(8,128)} %get-tuple-element.200, s32[16]{0:T(128)S(1)} %fusion.122, f32[16,3,577,128]{3,2,1,0:T(8,128)} %copy.187), kind=kCustom, calls=%fused_computation.3.clone.1 | custom fusion | flops 3545088 | bytes 42541120 | tf_op jit(solution)/shard_map/while/body/eval_jaxpr/scatter-add | solution.py:40
  428.0 10.2 copy.186
  438.2 7.3 broadcast_select_fusion.3
  455.2 19.7 %fusion.128 = f32[16,35,3,64]{3,1,2,0:T(8,128)} fusion(f32[16,3,35,577]{3,2,1,0:T(8,128)} %fusion.126, bf16[16,3,577,128]{2,3,1,0:T(8,128)(2,1)} %broadcast_select_fusion.3, f32[16,3,35,577]{3,2,1,0:T(8,128)} %get-tuple-element.189, f32[16,3,35]{2,1,0:T(4,128)S(1)} %get-tuple-element.190), kind=kOutput, calls=%fused_computation.26.clone.1 | convolution fusion | flops 130865856 | bytes 24088576 | tf_op jit(solution)/shard_map/while/body/eval_jaxpr/bhlk,bhkd->blhd/dot_general | solution.py:25
  479.8 20.3 %fusion.127 = f32[16,3,577,64]{2,3,1,0:T(8,128)} fusion(f32[16,3,35,577]{3,2,1,0:T(8,128)} %fusion.126, bf16[16,35,3,64]{3,2,0,1:T(4,128)(2,1)} %reshape.419, f32[16,3,35,577]{3,2,1,0:T(8,128)} %get-tuple-element.189, f32[16,3,35]{2,1,0:T(4,128)S(1)} %get-tuple-element.190), kind=kOutput, calls=%fused_computation.25.clone.1 | convolution fusion | flops 130865856 | bytes 15066816 | tf_op jit(solution)/shard_map/while/body/eval_jaxpr/bhlk,blhd->bhkd/dot_general | solution.py:26
  510.7 15.2 %copy.187 = f32[16,3,577,128]{3,2,1,0:T(8,128)} copy(f32[16,3,577,128]{2,3,1,0:T(8,128)} %pad_maximum_fusion.4) | data formatting | bytes 28360704 | tf_op jit(solution)/shard_map/while/body/eval_jaxpr/concatenate | solution.py:28
  525.9 29.9 %scatter_fusion = f32[4,3,577,128]{3,2,1,0:T(8,128)} fusion(f32[4,3,577,128]{3,2,1,0:T(8,128)} %get-tuple-element.200, s32[16]{0:T(128)S(1)} %fusion.122, f32[16,3,577,128]{3,2,1,0:T(8,128)} %copy.187), kind=kCustom, calls=%fused_computation.3.clone.1 | custom fusion | flops 3545088 | bytes 42541120 | tf_op jit(solution)/shard_map/while/body/eval_jaxpr/scatter-add | solution.py:40
  570.0 10.2 copy.186
  580.1 7.3 broadcast_select_fusion.3
  597.2 19.7 %fusion.128 = f32[16,35,3,64]{3,1,2,0:T(8,128)} fusion(f32[16,3,35,577]{3,2,1,0:T(8,128)} %fusion.126, bf16[16,3,577,128]{2,3,1,0:T(8,128)(2,1)} %broadcast_select_fusion.3, f32[16,3,35,577]{3,2,1,0:T(8,128)} %get-tuple-element.189, f32[16,3,35]{2,1,0:T(4,128)S(1)} %get-tuple-element.190), kind=kOutput, calls=%fused_computation.26.clone.1 | convolution fusion | flops 130865856 | bytes 24088576 | tf_op jit(solution)/shard_map/while/body/eval_jaxpr/bhlk,bhkd->blhd/dot_general | solution.py:25
  621.8 20.3 %fusion.127 = f32[16,3,577,64]{2,3,1,0:T(8,128)} fusion(f32[16,3,35,577]{3,2,1,0:T(8,128)} %fusion.126, bf16[16,35,3,64]{3,2,0,1:T(4,128)(2,1)} %reshape.419, f32[16,3,35,577]{3,2,1,0:T(8,128)} %get-tuple-element.189, f32[16,3,35]{2,1,0:T(4,128)S(1)} %get-tuple-element.190), kind=kOutput, calls=%fused_computation.25.clone.1 | convolution fusion | flops 130865856 | bytes 15066816 | tf_op jit(solution)/shard_map/while/body/eval_jaxpr/bhlk,blhd->bhkd/dot_general | solution.py:26
  652.7 15.2 %copy.187 = f32[16,3,577,128]{3,2,1,0:T(8,128)} copy(f32[16,3,577,128]{2,3,1,0:T(8,128)} %pad_maximum_fusion.4) | data formatting | bytes 28360704 | tf_op jit(solution)/shard_map/while/body/eval_jaxpr/concatenate | solution.py:28
  667.9 30.2 %scatter_fusion = f32[4,3,577,128]{3,2,1,0:T(8,128)} fusion(f32[4,3,577,128]{3,2,1,0:T(8,128)} %get-tuple-element.200, s32[16]{0:T(128)S(1)} %fusion.122, f32[16,3,577,128]{3,2,1,0:T(8,128)} %copy.187), kind=kCustom, calls=%fused_computation.3.clone.1 | custom fusion | flops 3545088 | bytes 42541120 | tf_op jit(solution)/shard_map/while/body/eval_jaxpr/scatter-add | solution.py:40
  712.2 10.2 copy.186
  722.3 7.3 broadcast_select_fusion.3
  739.4 19.7 %fusion.128 = f32[16,35,3,64]{3,1,2,0:T(8,128)} fusion(f32[16,3,35,577]{3,2,1,0:T(8,128)} %fusion.126, bf16[16,3,577,128]{2,3,1,0:T(8,128)(2,1)} %broadcast_select_fusion.3, f32[16,3,35,577]{3,2,1,0:T(8,128)} %get-tuple-element.189, f32[16,3,35]{2,1,0:T(4,128)S(1)} %get-tuple-element.190), kind=kOutput, calls=%fused_computation.26.clone.1 | convolution fusion | flops 130865856 | bytes 24088576 | tf_op jit(solution)/shard_map/while/body/eval_jaxpr/bhlk,bhkd->blhd/dot_general | solution.py:25
  764.0 20.3 %fusion.127 = f32[16,3,577,64]{2,3,1,0:T(8,128)} fusion(f32[16,3,35,577]{3,2,1,0:T(8,128)} %fusion.126, bf16[16,35,3,64]{3,2,0,1:T(4,128)(2,1)} %reshape.419, f32[16,3,35,577]{3,2,1,0:T(8,128)} %get-tuple-element.189, f32[16,3,35]{2,1,0:T(4,128)S(1)} %get-tuple-element.190), kind=kOutput, calls=%fused_computation.25.clone.1 | convolution fusion | flops 130865856 | bytes 15066816 | tf_op jit(solution)/shard_map/while/body/eval_jaxpr/bhlk,blhd->bhkd/dot_general | solution.py:26
  794.9 15.2 %copy.187 = f32[16,3,577,128]{3,2,1,0:T(8,128)} copy(f32[16,3,577,128]{2,3,1,0:T(8,128)} %pad_maximum_fusion.4) | data formatting | bytes 28360704 | tf_op jit(solution)/shard_map/while/body/eval_jaxpr/concatenate | solution.py:28
  810.1 29.3 %scatter_fusion = f32[4,3,577,128]{3,2,1,0:T(8,128)} fusion(f32[4,3,577,128]{3,2,1,0:T(8,128)} %get-tuple-element.200, s32[16]{0:T(128)S(1)} %fusion.122, f32[16,3,577,128]{3,2,1,0:T(8,128)} %copy.187), kind=kCustom, calls=%fused_computation.3.clone.1 | custom fusion | flops 3545088 | bytes 42541120 | tf_op jit(solution)/shard_map/while/body/eval_jaxpr/scatter-add | solution.py:40
  853.5 10.2 copy.186
  863.6 7.3 broadcast_select_fusion.3
  880.7 19.7 %fusion.128 = f32[16,35,3,64]{3,1,2,0:T(8,128)} fusion(f32[16,3,35,577]{3,2,1,0:T(8,128)} %fusion.126, bf16[16,3,577,128]{2,3,1,0:T(8,128)(2,1)} %broadcast_select_fusion.3, f32[16,3,35,577]{3,2,1,0:T(8,128)} %get-tuple-element.189, f32[16,3,35]{2,1,0:T(4,128)S(1)} %get-tuple-element.190), kind=kOutput, calls=%fused_computation.26.clone.1 | convolution fusion | flops 130865856 | bytes 24088576 | tf_op jit(solution)/shard_map/while/body/eval_jaxpr/bhlk,bhkd->blhd/dot_general | solution.py:25
  905.3 20.3 %fusion.127 = f32[16,3,577,64]{2,3,1,0:T(8,128)} fusion(f32[16,3,35,577]{3,2,1,0:T(8,128)} %fusion.126, bf16[16,35,3,64]{3,2,0,1:T(4,128)(2,1)} %reshape.419, f32[16,3,35,577]{3,2,1,0:T(8,128)} %get-tuple-element.189, f32[16,3,35]{2,1,0:T(4,128)S(1)} %get-tuple-element.190), kind=kOutput, calls=%fused_computation.25.clone.1 | convolution fusion | flops 130865856 | bytes 15066816 | tf_op jit(solution)/shard_map/while/body/eval_jaxpr/bhlk,blhd->bhkd/dot_general | solution.py:26
  936.2 15.2 %copy.187 = f32[16,3,577,128]{3,2,1,0:T(8,128)} copy(f32[16,3,577,128]{2,3,1,0:T(8,128)} %pad_maximum_fusion.4) | data formatting | bytes 28360704 | tf_op jit(solution)/shard_map/while/body/eval_jaxpr/concatenate | solution.py:28
  951.4 30.0 %scatter_fusion = f32[4,3,577,128]{3,2,1,0:T(8,128)} fusion(f32[4,3,577,128]{3,2,1,0:T(8,128)} %get-tuple-element.200, s32[16]{0:T(128)S(1)} %fusion.122, f32[16,3,577,128]{3,2,1,0:T(8,128)} %copy.187), kind=kCustom, calls=%fused_computation.3.clone.1 | custom fusion | flops 3545088 | bytes 42541120 | tf_op jit(solution)/shard_map/while/body/eval_jaxpr/scatter-add | solution.py:40
  1013.8 20.6 %gather_fusion.2 = bf16[16,3,577,128]{3,0,2,1:T(8,128)(2,1)} fusion(bf16[4,3,577,128]{3,0,2,1:T(4,128)(2,1)} %param.11, s32[1024]{0:T(1024)S(1)} %pad_clamp_fusion.2), kind=kCustom, calls=%fused_computation.1.clone | custom fusion | bytes 14180416 | tf_op jit(solution)/shard_map/while/body/eval_jaxpr/jit(_take)/gather | solution.py:38
  1034.4 10.9 copy.125
  1045.4 7.3 broadcast_select_fusion.1
  1062.3 20.0 %fusion.59 = f32[16,35,3,64]{3,1,2,0:T(8,128)} fusion(f32[16,3,35,577]{3,2,1,0:T(8,128)} %fusion.41, bf16[16,3,577,128]{2,3,1,0:T(8,128)(2,1)} %broadcast_select_fusion.1, f32[16,3,35,577]{3,2,1,0:T(8,128)} %get-tuple-element.135, f32[16,3,35]{2,1,0:T(4,128)S(1)} %get-tuple-element.134), kind=kOutput, calls=%fused_computation.70 | convolution fusion | flops 130865856 | bytes 24088576 | tf_op jit(solution)/shard_map/while/body/eval_jaxpr/bhlk,bhkd->blhd/dot_general | solution.py:25
  1104.3 21.0 %fusion.55 = f32[16,3,577,64]{2,3,1,0:T(8,128)} fusion(f32[16,3,35,577]{3,2,1,0:T(8,128)} %fusion.41, bf16[16,35,3,64]{3,2,1,0:T(4,128)(2,1)} %reshape.340, f32[16,3,35,577]{3,2,1,0:T(8,128)} %get-tuple-element.135, f32[16,3,35]{2,1,0:T(4,128)S(1)} %get-tuple-element.134), kind=kOutput, calls=%fused_computation.68 | convolution fusion | flops 130865856 | bytes 15066816 | tf_op jit(solution)/shard_map/while/body/eval_jaxpr/bhlk,blhd->bhkd/dot_general | solution.py:26
  1133.8 11.1 pad_maximum_fusion.1
  1144.9 15.2 %copy.150 = f32[16,3,577,128]{3,2,1,0:T(8,128)} copy(f32[16,3,577,128]{2,3,1,0:T(8,128)} %pad_maximum_fusion.1) | data formatting | bytes 28360704 | tf_op jit(solution)/shard_map/while/body/eval_jaxpr/concatenate | solution.py:28
  1160.2 28.9 %scatter_fusion.1 = f32[4,3,577,128]{3,2,1,0:T(8,128)} fusion(f32[4,3,577,128]{3,2,1,0:T(8,128)} %get-tuple-element.64, s32[16]{0:T(128)S(1)} %fusion.77, f32[16,3,577,128]{3,2,1,0:T(8,128)} %copy.150), kind=kCustom, calls=%fused_computation.4 | custom fusion | flops 3545088 | bytes 42541120 | tf_op jit(solution)/shard_map/while/body/eval_jaxpr/scatter-add | solution.py:40
  1195.1 10.1 all-reduce.2.cloned.1.call-done
  (233 shorter events, 358.6 us)
Async XLA Ops:
  8.0 28.1 %copy-start = (bf16[16,4,35,768]{3,1,2,0:T(4,128)(2,1)S(1)}, bf16[16,4,35,768]{3,1,2,0:T(4,128)(2,1)}, u32[]{:S(2)}) copy-start(bf16[16,4,35,768]{3,1,2,0:T(4,128)(2,1)} %param.12) | copy-start | bytes 10321924
  8.9 27.2 %copy-start.11 = (s32[16,3]{1,0:T(8,128)}, s32[16,3]{1,0:T(8,128)S(1)}, u32[]{:S(2)}) copy-start(s32[16,3]{1,0:T(8,128)S(1)} %copy.132) | copy-start | bytes 580
  9.4 26.7 %copy-start.14 = (s32[48]{0:T(128)}, s32[48]{0:T(128)S(1)}, u32[]{:S(2)}) copy-start(s32[48]{0:T(128)S(1)} %select_reduce_fusion.2) | copy-start | bytes 580
  10.2 42.7 %all-to-all-start = ((bf16[8,1,12]{2,1,0:T(2,128)(2,1)}), bf16[8,1,12]{2,1,0:T(2,128)(2,1)S(1)}, u32[]{:S(2)}, u32[]{:S(2)}) async-start(bf16[8,1,12]{2,1,0:T(2,128)(2,1)} %convert_element_type.81), calls=%async_computation | async-start | bytes 8192 | tf_op jit(solution)/shard_map/all_to_all | solution.py:95
  52.9 72.0 %all-to-all-start.1 = ((bf16[8,12,35,384]{3,2,1,0:T(8,128)(2,1)}), bf16[8,12,35,384]{3,2,1,0:T(8,128)(2,1)}, u32[]{:S(2)}, u32[]{:S(2)}) async-start(bf16[8,12,35,384]{3,2,1,0:T(8,128)(2,1)} %pad_maximum_fusion.2), calls=%async_computation.1 | async-start | bytes 5898240 | tf_op jit(solution)/shard_map/all_to_all | solution.py:94
  155.8 7.3 copy-start.3
  163.1 5.5 copy-start.1
  163.1 5.5 copy-start.4
  217.8 4.9 copy-start.2
  296.9 7.3 copy-start.3
  304.1 5.5 copy-start.1
  304.1 5.5 copy-start.4
  358.8 4.9 copy-start.2
  438.2 7.3 copy-start.3
  445.4 5.5 copy-start.1
  445.4 5.5 copy-start.4
  500.1 4.9 copy-start.2
  580.1 7.3 copy-start.3
  587.4 5.5 copy-start.1
  587.4 5.5 copy-start.4
  642.0 4.9 copy-start.2
  722.3 7.3 copy-start.3
  729.6 5.5 copy-start.1
  729.6 5.5 copy-start.4
  784.3 4.9 copy-start.2
  863.6 7.3 copy-start.3
  870.9 5.5 copy-start.1
  870.9 5.5 copy-start.4
  925.5 4.9 copy-start.2
  1000.8 5.8 copy-start.12
  1000.8 92.6 %all-to-all-start.2 = ((f32[8,12,35,192]{3,2,1,0:T(8,128)}), f32[8,12,35,192]{3,2,1,0:T(8,128)}, u32[]{:S(2)}, u32[]{:S(2)}) async-start(f32[8,12,35,192]{3,2,1,0:T(8,128)} %bitcast.51), calls=%async_computation.2 | async-start | bytes 7864320 | tf_op jit(solution)/shard_map/all_to_all | solution.py:103
  1006.6 186.6 %reduce-scatter.2.cloned.1.call-start = ((), (), s32[]{:S(2)}) async-start(), calls=%async_computation.4 | async-start | bytes 2457600 | tf_op jit(solution)/shard_map/reduce_scatter | solution.py:119
  1045.4 7.3 copy-start.6
  1052.6 5.5 copy-start.5
  1052.6 5.5 copy-start.7
  1062.3 25.0 %copy-start.15 = (s32[48]{0:T(128)S(1)}, s32[48]{0:T(128)}, u32[]{:S(2)}) copy-start(s32[48]{0:T(128)} %copy-done.14) | copy-start | bytes 580
  1082.3 15.3 %copy-start.13 = (pred[16,3]{1,0:T(8,128)(4,1)S(1)}, pred[16,3]{1,0:T(8,128)(4,1)}, u32[]{:S(2)}) copy-start(pred[16,3]{1,0:T(8,128)(4,1)} %get-tuple-element.124) | copy-start | bytes 148
  1100.6 0.7 copy-start.8
  1104.0 101.2 %all-reduce.2.cloned.1.call-start = ((), (), s32[]{:S(2)}) async-start(), calls=%async_computation.5 | async-start | bytes 1179648 | tf_op jit(solution)/shard_map/psum | solution.py:117
  1125.3 7.1 copy-start.9
  1125.3 7.1 copy-start.10
Sparse Core Ops, SparseCore 0:
  1104.1 29.7 reduce-scatter.1
Sparse Core Ops, SparseCore 1:
  1133.9 71.2 all-reduce.1
where the time goes:
time: 1230 us; the launch traced here: 1220 us
  local copies, waits for them, and re-layouts  381 us (31%)
  matrix products  369 us (30%)
  other arithmetic  339 us (28%)
  waiting for transfers between devices  79.4 us (6%)
  starting transfers between devices  19.4 us (2%)
  between operations  16.1 us (1%)
    scatter-add x7, other arithmetic, visit(): memory_acc = memory_acc.at[ids].add(pair_dkv)  207 us
    dot_general x7, matrix products, pair_grads(): jnp.einsum('bhlk,blhd->bhkd', dscores, q4, preferred_element_type=jnp.flo...  143 us
    dot_general x7, matrix products, pair_grads(): jnp.einsum('bhlk,bhkd->blhd', dscores, k4, preferred_element_type=jnp.flo...  138 us
    gather x14, local copies, waits for them, and re-layouts, visit(): memory = jnp.take(patch_key_value, ids, axis=0)  128 us
    concatenate x7, local copies, waits for them, and re-layouts, pair_grads(): return (pair_dq, jnp.concatenate([pair_dk, pair_dv], axis=-1))  106 us
    all_to_all x1, waiting for transfers between devices, per_device(): lax.all_to_all(send_pair, 'dp', split_axis=0, concat_axis=0, tiled=True)  63 us
    select_n x8, other arithmetic, visit(): memory = jnp.take(patch_key_value, ids, axis=0)  50.8 us
    concatenate x7, other arithmetic, pair_grads(): return (pair_dq, jnp.concatenate([pair_dk, pair_dv], axis=-1))  45.9 us
  transfers between devices with their start and end apart: 5, of which 3 were waited for; matrix products, arithmetic and copies ran while one was open for 17% of the time, Pallas kernels for 0%

commit v1 on v0

v1 whole, which is shorter than its diff:
```python
import functools

import jax
import jax.numpy as jnp
from jax import lax
from jax.experimental import pallas as pl
from jax.experimental.pallas import tpu as pltpu
from jax.sharding import PartitionSpec as P

HEAD_SIZE = 64
NEG = 3
F32 = jnp.float32
BF16 = jnp.bfloat16
NN = (((1,), (0,)), ((), ()))
NT = (((1,), (1,)), ((), ()))
TN = (((0,), (0,)), ((), ()))


def dot(a, b, dims=NN):
    return lax.dot_general(a, b, dims, preferred_element_type=F32)


def attend(h, chunk, mask, hot, km, vm, kmt, dk, dv, images):
    scale = HEAD_SIZE ** (-0.5)
    zero = jnp.zeros((), BF16)
    qm = jnp.where(mask, jnp.concatenate([chunk[:, :HEAD_SIZE]] * images, axis=1), zero)
    gm = jnp.where(mask, jnp.concatenate([chunk[:, HEAD_SIZE:]] * images, axis=1), zero)
    scores = dot(km[h], qm, NT)
    top = jnp.max(scores, axis=0, keepdims=True)
    e = jnp.exp((scores - top) * scale)
    probs = e * (1.0 / jnp.sum(e, axis=0, keepdims=True))
    dprobs = dot(vm[h], gm, NT)
    center = jnp.sum(probs * dprobs, axis=0, keepdims=True)
    ds = (probs * ((dprobs - center) * scale)).astype(BF16)
    dv[h] += dot(probs.astype(BF16), gm)
    dk[h] += dot(ds, qm)
    wide = dot(kmt[h], ds)
    out = hot[0:1, :] * wide[:HEAD_SIZE]
    for i in range(1, images):
        out += hot[i : i + 1, :] * wide[i * HEAD_SIZE : (i + 1) * HEAD_SIZE]
    return out.T


def kernel(
    n, heads, images, captions, length,
    texts, weight, g_own, g_neg, km, vm, kmt, src_col, srcq_col, srcq_row, ids,
    dq_out, kv_out,
    q_s, own_s, send, recv, idrecv, ret, retrecv, dk, dv, dq_s,
    send_sem, recv_sem, id_send, id_recv, ret_send, ret_recv,
):
    me = lax.axis_index("dp")
    tokens = texts.shape[0]
    count = src_col.shape[1]
    wanted = g_neg.shape[0]
    wide = images * HEAD_SIZE

    barrier = pltpu.get_barrier_semaphore()

    def greet(d, c):
        pl.semaphore_signal(
            barrier, inc=1, device_id={"dp": lax.rem(me + d, n)}, device_id_type=pl.DeviceIdType.MESH
        )
        return c

    lax.fori_loop(1, n, greet, 0)

    def chunk_copy(d):
        return pltpu.make_async_remote_copy(
            src_ref=send.at[d], dst_ref=recv.at[d], send_sem=send_sem.at[d], recv_sem=recv_sem.at[d],
            device_id={"dp": lax.rem(me + d, n)}, device_id_type=pl.DeviceIdType.MESH,
        )

    def id_copy(d):
        to = lax.rem(me + d, n)
        return pltpu.make_async_remote_copy(
            src_ref=ids.at[to], dst_ref=idrecv.at[d], send_sem=id_send.at[d], recv_sem=id_recv.at[d],
            device_id={"dp": to}, device_id_type=pl.DeviceIdType.MESH,
        )

    def ret_copy(d):
        return pltpu.make_async_remote_copy(
            src_ref=ret.at[d], dst_ref=retrecv.at[d], send_sem=ret_send.at[d], recv_sem=ret_recv.at[d],
            device_id={"dp": lax.rem(me + n - d, n)}, device_id_type=pl.DeviceIdType.MESH,
        )

    q_s[...] = dot(texts[...], weight[...], NT).astype(BF16)
    pl.semaphore_wait(barrier, n - 1)

    def pack(d, c):
        to = lax.rem(me + d, n)
        hot_g = (src_col[to] == lax.broadcasted_iota(jnp.int32, (count, wanted), 1)).astype(F32).astype(BF16)
        hot_q = (srcq_col[to] == lax.broadcasted_iota(jnp.int32, (count, tokens), 1)).astype(F32).astype(BF16)
        pq = dot(hot_q, q_s[...]).astype(BF16)
        pg = dot(hot_g, g_neg[...]).astype(BF16)
        for h in range(heads):
            cols = slice(h * HEAD_SIZE, (h + 1) * HEAD_SIZE)
            send[d, h] = jnp.concatenate([pq[:, cols], pg[:, cols]], axis=1)
        chunk_copy(d).start()
        id_copy(d).start()
        return c

    lax.fori_loop(1, n, pack, 0)

    dk[...] = jnp.zeros_like(dk)
    dv[...] = jnp.zeros_like(dv)
    qv, gv = q_s[...], g_own[...]
    for h in range(heads):
        cols = slice(h * HEAD_SIZE, (h + 1) * HEAD_SIZE)
        own_s[h] = jnp.concatenate([qv[:, cols], gv[:, cols]], axis=1)

    per_image = captions * length
    own_mask = (
        lax.broadcasted_iota(jnp.int32, (tokens, wide), 0) // per_image
        == lax.broadcasted_iota(jnp.int32, (tokens, wide), 1) // HEAD_SIZE
    )
    own_hot = (
        lax.broadcasted_iota(jnp.int32, (16, tokens), 1) // per_image
        == lax.broadcasted_iota(jnp.int32, (16, tokens), 0)
    ).astype(F32)

    def own_head(h, c):
        dq = attend(h, own_s[h], own_mask, own_hot, km, vm, kmt, dk, dv, images)
        hi = dq.astype(BF16)
        dq_s[h] = jnp.concatenate([dq, jnp.zeros_like(dq)], axis=1)
        return c

    lax.fori_loop(0, heads, own_head, 0)

    spread = (
        lax.broadcasted_iota(jnp.int32, (16, wide), 0)
        == lax.broadcasted_iota(jnp.int32, (16, wide), 1) // HEAD_SIZE
    ).astype(F32).astype(BF16)

    def serve(d, c):
        chunk_copy(d).wait_recv()
        id_copy(d).wait_recv()
        hot = idrecv[d]
        mask = dot(hot, spread, TN) > 0.5
        hot = hot.astype(F32)

        def head(h, c2):
            dq = attend(h, recv[d, h], mask, hot, km, vm, kmt, dk, dv, images)
            hi = dq.astype(BF16)
            lo = (dq - hi.astype(F32)).astype(BF16)
            ret[d, h] = jnp.concatenate([hi, lo], axis=1)
            return c2

        lax.fori_loop(0, heads, head, 0)
        ret_copy(d).start()
        return c

    lax.fori_loop(1, n, serve, 0)

    for h in range(heads):
        for i in range(images):
            cols = slice(i * HEAD_SIZE, (i + 1) * HEAD_SIZE)
            kv_out[i, h] = jnp.concatenate([dk[h, :, cols], dv[h, :, cols]], axis=1).astype(BF16)

    def collect(d, c):
        ret_copy(d).wait_recv()
        row = srcq_row[lax.rem(me + d, n)][0:1, :]
        hot = (row == lax.broadcasted_iota(jnp.int32, (tokens, count), 0)).astype(F32).astype(BF16)

        def head(h, c2):
            dq_s[h] += dot(hot, retrecv[d, h])
            return c2

        lax.fori_loop(0, heads, head, 0)
        return c

    lax.fori_loop(1, n, collect, 0)
    parts = [dq_s[h, :, :HEAD_SIZE] + dq_s[h, :, HEAD_SIZE:] for h in range(heads)]
    dq_out[...] = jnp.concatenate(parts, axis=1).astype(BF16)

    def drain(d, c):
        chunk_copy(d).wait_send()
        id_copy(d).wait_send()
        ret_copy(d).wait_send()
        return c

    lax.fori_loop(1, n, drain, 0)


def per_device(texts, query_weight, patch_key_value, grad_out, negatives):
    n = lax.axis_size("dp")
    texts_here, length, _ = texts.shape
    images, heads, patches, _ = patch_key_value.shape
    captions = texts_here // images
    wanted = NEG * texts_here
    capacity = 2 * max(1, wanted // n)
    width = query_weight.shape[0]
    tokens = texts_here * length
    count = -(-(capacity * length) // 16) * 16
    flat_text = texts.reshape(tokens, -1)
    grad_cols = lax.dynamic_slice_in_dim(grad_out, lax.axis_index("mp") * width, width, 3)
    g_own = grad_cols[:, 0].reshape(tokens, width)
    g_neg = grad_cols[:, 1:].reshape(wanted * length, width)

    flat_neg = negatives.reshape(-1)
    owner = flat_neg // images
    owner_hot = (owner[:, None] == jnp.arange(n, dtype=jnp.int32)[None, :]).astype(jnp.int32)
    earlier = jnp.cumsum(owner_hot, axis=0) - owner_hot
    rank = jnp.sum(earlier * owner_hot, axis=1)
    slot = owner * capacity + rank
    placed = slot[None, :] == jnp.arange(n * capacity, dtype=jnp.int32)[:, None]
    used = jnp.any(placed, axis=1)
    pair = jnp.sum(jnp.where(placed, jnp.arange(wanted, dtype=jnp.int32)[None, :], 0), axis=1)
    image = jnp.sum(jnp.where(placed, (flat_neg % images)[None, :], 0), axis=1)

    def per_token(start):
        rows = start[:, None] + jnp.arange(length, dtype=jnp.int32)[None, :]
        rows = jnp.where(used[:, None], rows, -1).reshape(n, capacity * length)
        return jnp.pad(rows, ((0, 0), (0, count - capacity * length)), constant_values=-1)

    src = per_token(pair * length)
    srcq = per_token((pair // NEG) * length)
    image_rows = jnp.broadcast_to(jnp.where(used, image, -1)[:, None], (n * capacity, length))
    image_rows = jnp.pad(
        image_rows.reshape(n, capacity * length),
        ((0, 0), (0, count - capacity * length)), constant_values=-1,
    )
    ids = (image_rows[:, None, :] == jnp.arange(16, dtype=jnp.int32)[None, :, None]).astype(BF16)
    srcq_row = jnp.broadcast_to(srcq[:, None, :], (n, 8, count))

    wide = images * HEAD_SIZE
    km = patch_key_value[..., :HEAD_SIZE].transpose(1, 2, 0, 3).reshape(heads, patches, wide)
    vm = patch_key_value[..., HEAD_SIZE:].transpose(1, 2, 0, 3).reshape(heads, patches, wide)
    kmt = km.transpose(0, 2, 1)

    vmem = pl.BlockSpec(memory_space=pltpu.VMEM)
    box = (n, heads, count, 2 * HEAD_SIZE)
    dma = pltpu.SemaphoreType.DMA((n,))
    dquery, key_value_grad = pl.pallas_call(
        functools.partial(kernel, n, heads, images, captions, length),
        out_shape=(
            jax.ShapeDtypeStruct((tokens, width), BF16),
            jax.ShapeDtypeStruct(patch_key_value.shape, BF16),
        ),
        in_specs=[vmem] * 11,
        out_specs=(vmem, vmem),
        scratch_shapes=[
            pltpu.VMEM((tokens, width), BF16),
            pltpu.VMEM((heads, tokens, 2 * HEAD_SIZE), BF16),
            pltpu.VMEM(box, BF16),
            pltpu.VMEM(box, BF16),
            pltpu.VMEM((n, 16, count), BF16),
            pltpu.VMEM(box, BF16),
            pltpu.VMEM(box, BF16),
            pltpu.VMEM((heads, patches, wide), F32),
            pltpu.VMEM((heads, patches, wide), F32),
            pltpu.VMEM((heads, tokens, 2 * HEAD_SIZE), F32),
            dma, dma, dma, dma, dma, dma,
        ],
        compiler_params=pltpu.CompilerParams(
            collective_id=0, has_side_effects=True, vmem_limit_bytes=60 * 1024 * 1024
        ),
    )(
        flat_text, query_weight, g_own, g_neg, km, vm, kmt,
        src[:, :, None], srcq[:, :, None], srcq_row, ids,
    )

    weight_local = dot(dquery, flat_text, TN)
    weight_grad = lax.psum(weight_local, "dp")
    text_term = dot(dquery, query_weight)
    text_grad = lax.psum_scatter(
        text_term.reshape(texts_here, length, -1), "mp", scatter_dimension=0, tiled=True
    )
    return (text_grad.astype(BF16), weight_grad, key_value_grad)


def solution(mesh):
    in_specs = (
        P("dp", None, None),
        P("mp", None),
        P("dp", "mp", None, None),
        P("dp", None, None, None),
        P("dp", None),
    )
    out_specs = (P(("dp", "mp"), None, None), P("mp", None), P("dp", "mp", None, None))
    return jax.shard_map(
        per_device, mesh=mesh, in_specs=in_specs, out_specs=out_specs, check_vma=False
    )
```

time: 1230 us -> 285 us (0.23); the launches traced: 1220 us -> 285 us
  matrix products: 369 us -> 5.02 us
  other arithmetic: 339 us -> 3.02 us
  local copies, waits for them, and re-layouts: 381 us -> 47.8 us
  Pallas kernels: 0 us -> 146 us
  starting transfers between devices: 19.4 us -> 0.08 us
  waiting for transfers between devices: 79.4 us -> 66.8 us
    dot_general x40 -> x2, matrix products: 369 us -> 5.02 us  [dot(): return lax.dot_general(a, b, dims, preferred_element_type=F32)]
    scatter-add x7 -> x0, other arithmetic: 207 us -> none  [visit(): memory_acc = memory_acc.at[ids].add(pair_dkv)]
    pallas_call x0 -> x1, Pallas kernels: none -> 146 us  [per_device(): pl.pallas_call(functools.partial(kernel, n, heads, images, captions, leng...]
    gather x15 -> x0, local copies, waits for them, and re-layouts: 132 us -> none  [the longest x14 128 us: visit(): memory = jnp.take(patch_key_value, ids, axis=0)]
    concatenate x7 -> x0, local copies, waits for them, and re-layouts: 106 us -> none  [pair_grads(): return (pair_dq, jnp.concatenate([pair_dk, pair_dv], axis=-1))]
    all_to_all x3 -> x0, waiting for transfers between devices: 69.2 us -> none  [the longest x1 63 us: per_device(): lax.all_to_all(send_pair, 'dp', split_axis=0, concat_axis=0, tiled=True)]
    concatenate x8 -> x0, other arithmetic: 50.7 us -> none  [the longest x7 45.9 us: pair_grads(): return (pair_dq, jnp.concatenate([pair_dk, pair_dv], axis=-1))]
    select_n x17 -> x3, other arithmetic: 50.8 us -> 0.72 us  [the longest x1 0.71 us: per_token(): rows = jnp.where(used[:, None], rows, -1).reshape(n, capacity * length)]
  transfers between devices with their start and end apart: 5 -> 2, of which waited for: 3 -> 2; matrix products, arithmetic and copies ran while one was open for 17% -> 3% of each run, Pallas kernels for 0% -> 0%
where the time goes in v1:
time: 285 us
  Pallas kernels  146 us (51%)
  waiting for transfers between devices  66.8 us (23%)
  local copies, waits for them, and re-layouts  47.8 us (17%)
  between operations  15.6 us (5%)
  matrix products  5.02 us (2%)
  other arithmetic  3.02 us (1%)
    pallas_call x1, Pallas kernels, per_device(): pl.pallas_call(functools.partial(kernel, n, heads, images, captions, leng...  146 us
    psum x1, waiting for transfers between devices, per_device(): weight_grad = lax.psum(weight_local, 'dp')  44.7 us
    reduce_scatter x1, waiting for transfers between devices, per_device(): lax.psum_scatter(text_term.reshape(texts_here, length, -1), 'mp', scatter...  22.1 us
    unnamed x9, local copies, waits for them, and re-layouts  9.37 us
    transpose x2, local copies, waits for them, and re-layouts, per_device(): patch_key_value[..., HEAD_SIZE:].transpose(1, 2, 0, 3)  8.92 us
  transfers between devices with their start and end apart: 2, of which 2 were waited for; matrix products, arithmetic and copies ran while one was open for 3% of the time, Pallas kernels for 0%

profile of v1, /device:TPU:0, one launch (start us, length us, event | category | flops | bytes accessed | tf_op | source)
XLA Modules:
  0.0 284.8 jit_solution(8653564177245169668)
XLA Ops:
  8.1 0.9 copy.41
  9.0 0.1 reshape.166
  9.1 0.1 fusion.2
  9.1 0.1 reduce_window_sum.11
  9.2 0.2 select_reduce_fusion.2
  9.4 0.1 fusion.1
  9.5 0.1 select_reduce_fusion
  9.7 0.7 add.89
  10.3 0.1 broadcast_in_dim.74
  10.4 0.1 and.47
  10.5 0.1 div.30
  10.6 0.1 reduce_sum.32
  10.7 0.1 mul.38
  10.7 0.1 broadcast_in_dim.75
  10.8 0.7 broadcast_in_dim.76
  11.5 0.1 add.86
  11.6 0.1 add.87
  11.7 0.1 broadcast_in_dim.84
  11.8 0.1 broadcast_in_dim.85
  11.9 0.1 add.92
  12.0 0.1 add.93
  12.1 0.7 add_select_fusion
  12.8 0.7 fusion.ids
  13.5 2.8 dynamic-slice_reduce_fusion
  16.3 1.8 reshape_squeeze.3.g_own
  18.1 2.4 copy.37
  20.4 2.4 reshape.162.texts
  22.8 1.2 constant_dynamic-slice_fusion
  24.0 1.1 copy.38
  25.1 2.3 reshape.163.g_neg
  27.4 1.8 copy.44.src_col
  29.2 1.8 copy.45.srcq_col
  31.1 5.3 %slice_bitcast_fusion = (bf16[3,577,4,64]{3,2,1,0:T(4,128)(2,1)}, bf16[3,577,4,64]{3,2,1,0:T(4,128)(2,1)}) fusion(bf16[4,3,577,128]{3,0,2,1:T(4,128)(2,1)} %param.7), kind=kLoop, calls=%fused_computation | loop fusion | bytes 3545088 | tf_op jit(solution)/shard_map/transpose | solution.py:227
  36.4 3.6 %copy.40 = bf16[3,577,4,64]{1,3,2,0:T(8,128)(2,1)} copy(bf16[3,577,4,64]{3,2,1,0:T(4,128)(2,1)} %get-tuple-element.21) | data formatting | bytes 1772544 | tf_op jit(solution)/shard_map/transpose | solution.py:227
  40.0 2.3 copy.43.vm
  42.3 3.6 %copy.39 = bf16[3,577,4,64]{1,3,2,0:T(8,128)(2,1)} copy(bf16[3,577,4,64]{3,2,1,0:T(4,128)(2,1)} %get-tuple-element.22) | data formatting | bytes 1772544 | tf_op jit(solution)/shard_map/transpose | solution.py:226
  45.9 2.3 copy.42.km
  48.2 0.7 broadcast_in_dim.82.srcq_row
  48.8 146.4 %shard_map.76 = (bf16[560,192]{1,0:T(8,128)(2,1)}, bf16[4,3,577,128]{3,2,1,0:T(8,128)(2,1)}) custom-call(bf16[560,768]{1,0:T(8,128)(2,1)} %reshape.162.texts, bf16[192,768]{1,0:T(8,128)(2,1)} %weight.1, bf16[560,192]{1,0:T(8,128)(2,1)} %reshape_squeeze.3.g_own, bf16[1680,192]{1,0:T(8,128)(2,1)} %reshape.163.g_neg, bf16[3,577,256]{2,1,0:T(8,128)(2,1)} %copy.42.km, ...), custom_call_target="tpu_custom_call" | custom-call | tf_op jit(solution)/shard_map/pallas_call | solution.py:233
  195.3 2.5 fusion.5
  197.8 3.0 %reshape.167 = f32[16,35,768]{2,1,0:T(8,128)} reshape(f32[560,768]{1,0:T(8,128)} %fusion.5) | data formatting | bytes 3440640 | tf_op jit(solution)/shard_map/reshape | solution.py:266
  200.9 2.5 fusion.6
  203.4 3.4 %copy.47 = bf16[4,3,577,128]{3,0,2,1:T(4,128)(2,1)} copy(bf16[4,3,577,128]{3,2,1,0:T(8,128)(2,1)} %get-tuple-element.18) | data formatting | bytes 3545088
  206.8 22.1 %reduce-scatter.2.cloned.1.call-done = f32[4,35,768]{2,1,0:T(8,128)} async-done(((f32[16,35,768]{2,1,0:T(8,128)}), f32[4,35,768]{2,1,0:T(8,128)}) %reduce-scatter.2.cloned.1.call-update) | async-done | bytes 430096 | tf_op jit(solution)/shard_map/reduce_scatter | solution.py:265
  228.9 1.1 convert_element_type.11
  230.0 0.8 copy.46
  230.7 44.7 %all-reduce.5.cloned.1.call-done = f32[192,768]{1,0:T(8,128)} async-done(((f32[192,768]{1,0:T(8,128)}), f32[192,768]{1,0:T(8,128)}) %all-reduce.5.cloned.1.call-update) | async-done | bytes 589840 | tf_op jit(solution)/shard_map/psum | solution.py:263
  275.4 1.9 copy.50
  (18 shorter events, 0.2 us)
Async XLA Ops:
  8.0 5.5 %copy-start = (bf16[16,4,35,768]{3,1,2,0:T(4,128)(2,1)S(1)}, bf16[16,4,35,768]{3,1,2,0:T(4,128)(2,1)}, u32[]{:S(2)}) copy-start(bf16[16,4,35,768]{3,1,2,0:T(4,128)(2,1)} %param.8) | copy-start | bytes 10321924
  8.0 220.9 %reduce-scatter.2.cloned.1.call-start = ((), (), s32[]{:S(2)}) async-start(), calls=%async_computation.1 | async-start | bytes 2457600 | tf_op jit(solution)/shard_map/reduce_scatter | solution.py:265
  48.8 146.4 %copy-start.1 = (bf16[192,768]{1,0:T(8,128)(2,1)S(1)}, bf16[192,768]{1,0:T(8,128)(2,1)}, u32[]{:S(2)}) copy-start(bf16[192,768]{1,0:T(8,128)(2,1)} %weight.1) | copy-start | bytes 884740
  200.8 74.6 %all-reduce.5.cloned.1.call-start = ((), (), s32[]{:S(2)}) async-start(), calls=%async_computation.2 | async-start | bytes 1179648 | tf_op jit(solution)/shard_map/psum | solution.py:263
Sparse Core Ops, SparseCore 0:
  200.9 27.9 reduce-scatter.1
Sparse Core Ops, SparseCore 1:
  205.6 69.7 all-reduce.4

commit v2 on v1

v2 whole, which is shorter than its diff:
```python
import functools

import jax
import jax.numpy as jnp
from jax import lax
from jax.experimental import pallas as pl
from jax.experimental.pallas import tpu as pltpu
from jax.sharding import PartitionSpec as P

HEAD_SIZE = 64
NEG = 3
F32 = jnp.float32
BF16 = jnp.bfloat16
NN = (((1,), (0,)), ((), ()))
NT = (((1,), (1,)), ((), ()))
TN = (((0,), (0,)), ((), ()))


def dot(a, b, dims=NN):
    return lax.dot_general(a, b, dims, preferred_element_type=F32)


def attend(h, chunk, mask, hot, km, vm, kmt, dk, dv, images):
    scale = HEAD_SIZE ** (-0.5)
    zero = jnp.zeros((), BF16)
    qm = jnp.where(mask, jnp.concatenate([chunk[:, :HEAD_SIZE]] * images, axis=1), zero)
    gm = jnp.where(mask, jnp.concatenate([chunk[:, HEAD_SIZE:]] * images, axis=1), zero)
    scores = dot(km[h], qm, NT)
    top = jnp.max(scores, axis=0, keepdims=True)
    e = jnp.exp((scores - top) * scale)
    probs = e * (1.0 / jnp.sum(e, axis=0, keepdims=True))
    dprobs = dot(vm[h], gm, NT)
    center = jnp.sum(probs * dprobs, axis=0, keepdims=True)
    ds = (probs * ((dprobs - center) * scale)).astype(BF16)
    dv[h] += dot(probs.astype(BF16), gm)
    dk[h] += dot(ds, qm)
    wide = dot(kmt[h], ds)
    out = hot[0:1, :] * wide[:HEAD_SIZE]
    for i in range(1, images):
        out += hot[i : i + 1, :] * wide[i * HEAD_SIZE : (i + 1) * HEAD_SIZE]
    return out.T


def kernel(
    n, m, heads, images, captions, length,
    texts, weight, grads, kv, rows,
    text_out, weight_out, kv_out,
    q_s, own_s, send, recv, rowrecv, ret, retrecv, km, vm, kmt, pad_s, dk, dv, dq_s, dqf_s,
    dq_send, dq_recv, w_recv, part_s, part_recv, sum_s, sum_recv,
    send_sem, recv_sem, id_send, id_recv, ret_send, ret_recv, part_ss, part_rs, sum_ss, sum_rs,
    w_ss, w_rs, dq_ss, dq_rs,
):
    me, mine = lax.axis_index("dp"), lax.axis_index("mp")
    tokens = texts.shape[0]
    count = send.shape[2]
    total = grads.shape[0]
    wide = images * HEAD_SIZE
    patches = kv.shape[2]
    share = dq_send.shape[1]
    piece = tokens // m
    band = part_recv.shape[1]
    bands = weight.shape[0] // band
    mesh_id = pl.DeviceIdType.MESH

    barrier = pltpu.get_barrier_semaphore()

    def greet_dp(d, c):
        pl.semaphore_signal(
            barrier, inc=1, device_id={"dp": lax.rem(me + d, n)}, device_id_type=mesh_id
        )
        return c

    def greet_mp(d, c):
        pl.semaphore_signal(
            barrier, inc=1, device_id={"mp": lax.rem(mine + d, m)}, device_id_type=mesh_id
        )
        return c

    lax.fori_loop(1, n, greet_dp, 0)
    lax.fori_loop(1, m, greet_mp, 0)

    def dp_copy(src, dst, ss, rs, to):
        return pltpu.make_async_remote_copy(
            src_ref=src, dst_ref=dst, send_sem=ss, recv_sem=rs, device_id={"dp": to}, device_id_type=mesh_id
        )

    def mp_copy(src, dst, ss, rs, to):
        return pltpu.make_async_remote_copy(
            src_ref=src, dst_ref=dst, send_sem=ss, recv_sem=rs, device_id={"mp": to}, device_id_type=mesh_id
        )

    def chunk_copy(d):
        return dp_copy(send.at[d], recv.at[d], send_sem.at[d], recv_sem.at[d], lax.rem(me + d, n))

    def row_copy(d):
        to = lax.rem(me + d, n)
        return dp_copy(rows.at[to], rowrecv.at[d], id_send.at[d], id_recv.at[d], to)

    def ret_copy(d):
        return dp_copy(ret.at[d], retrecv.at[d], ret_send.at[d], ret_recv.at[d], lax.rem(me + n - d, n))

    def part_copy(d):
        to = lax.rem(me + d, n)
        at = pl.ds(pl.multiple_of(lax.rem(to, bands) * band, 8), band)
        return dp_copy(part_s.at[at], part_recv.at[d], part_ss.at[d], part_rs.at[d], to)

    def sum_copy(d):
        return dp_copy(sum_s, sum_recv.at[d], sum_ss.at[d], sum_rs.at[d], lax.rem(me + d, n))

    def w_copy(d):
        return mp_copy(weight, w_recv.at[d], w_ss.at[d], w_rs.at[d], lax.rem(mine + d, m))

    def dq_copy(d):
        to = lax.rem(mine + d, m)
        return mp_copy(dq_send.at[to], dq_recv.at[d], dq_ss.at[d], dq_rs.at[d], to)

    q_s[...] = dot(texts[...], weight[...], NT).astype(BF16)
    pl.semaphore_wait(barrier, n + m - 2)

    def pack(d, c):
        to = lax.rem(me + d, n)
        columns = rows[to].T[:count].astype(jnp.int32)
        hot_g = (columns[:, 0:1] == lax.broadcasted_iota(jnp.int32, (count, total), 1)).astype(F32).astype(BF16)
        hot_q = (columns[:, 1:2] == lax.broadcasted_iota(jnp.int32, (count, tokens), 1)).astype(F32).astype(BF16)
        pq = dot(hot_q, q_s[...]).astype(BF16)
        pg = dot(hot_g, grads[...]).astype(BF16)
        for h in range(heads):
            cols = slice(h * HEAD_SIZE, (h + 1) * HEAD_SIZE)
            send[d, h] = jnp.concatenate([pq[:, cols], pg[:, cols]], axis=1)
        chunk_copy(d).start()
        row_copy(d).start()
        return c

    lax.fori_loop(1, n, pack, 0)

    def send_w(d, c):
        w_copy(d).start()
        return c

    lax.fori_loop(1, m, send_w, 0)

    pad_s[...] = jnp.zeros_like(pad_s)
    for h in range(heads):
        keys = jnp.concatenate([kv[i, h, :, :HEAD_SIZE] for i in range(images)], axis=1)
        km[h] = keys
        vm[h] = jnp.concatenate([kv[i, h, :, HEAD_SIZE:] for i in range(images)], axis=1)
        pad_s[:patches] = keys
        kmt[h] = pad_s[...].T[:, :patches]
    dk[...] = jnp.zeros_like(dk)
    dv[...] = jnp.zeros_like(dv)
    qv, gv = q_s[...], grads[:tokens]
    for h in range(heads):
        cols = slice(h * HEAD_SIZE, (h + 1) * HEAD_SIZE)
        own_s[h] = jnp.concatenate([qv[:, cols], gv[:, cols]], axis=1)

    per_image = captions * length
    own_mask = (
        lax.broadcasted_iota(jnp.int32, (tokens, wide), 0) // per_image
        == lax.broadcasted_iota(jnp.int32, (tokens, wide), 1) // HEAD_SIZE
    )
    own_hot = (
        lax.broadcasted_iota(jnp.int32, (16, tokens), 1) // per_image
        == lax.broadcasted_iota(jnp.int32, (16, tokens), 0)
    ).astype(F32)

    def own_head(h, c):
        dq = attend(h, own_s[h], own_mask, own_hot, km, vm, kmt, dk, dv, images)
        dq_s[h] = jnp.concatenate([dq, jnp.zeros_like(dq)], axis=1)
        return c

    lax.fori_loop(0, heads, own_head, 0)

    spread = (
        lax.broadcasted_iota(jnp.int32, (16, wide), 0)
        == lax.broadcasted_iota(jnp.int32, (16, wide), 1) // HEAD_SIZE
    ).astype(F32).astype(BF16)

    def serve(d, c):
        chunk_copy(d).wait_recv()
        row_copy(d).wait_recv()
        named = rowrecv[d][2:3, :count].astype(jnp.int32)
        hot = (named == lax.broadcasted_iota(jnp.int32, (16, count), 0)).astype(F32)
        mask = dot(hot.astype(BF16), spread, TN) > 0.5

        def head(h, c2):
            dq = attend(h, recv[d, h], mask, hot, km, vm, kmt, dk, dv, images)
            hi = dq.astype(BF16)
            lo = (dq - hi.astype(F32)).astype(BF16)
            ret[d, h] = jnp.concatenate([hi, lo], axis=1)
            return c2

        lax.fori_loop(0, heads, head, 0)
        ret_copy(d).start()
        return c

    lax.fori_loop(1, n, serve, 0)

    def collect(d, c):
        ret_copy(d).wait_recv()
        row = rows[lax.rem(me + d, n)][1:2, :count].astype(jnp.int32)
        hot = (row == lax.broadcasted_iota(jnp.int32, (tokens, count), 0)).astype(F32).astype(BF16)

        def head(h, c2):
            dq_s[h] += dot(hot, retrecv[d, h])
            return c2

        lax.fori_loop(0, heads, head, 0)
        return c

    lax.fori_loop(1, n, collect, 0)
    parts = [dq_s[h, :, :HEAD_SIZE] + dq_s[h, :, HEAD_SIZE:] for h in range(heads)]
    dqf_s[...] = jnp.concatenate(parts, axis=1)
    dq_send[...] = jnp.zeros_like(dq_send)
    for j in range(m):
        dq_send[j, :piece] = dqf_s[j * piece : (j + 1) * piece].astype(BF16)

    def send_dq(d, c):
        dq_copy(d).start()
        return c

    lax.fori_loop(1, m, send_dq, 0)
    part_s[...] = dot(dqf_s[...].astype(BF16), texts[...], TN)

    def if_band(who, f):
        if bands == n:
            f()
        else:
            pl.when(who < bands)(f)

    def send_part(d, c):
        if_band(lax.rem(me + d, n), lambda: part_copy(d).start())
        return c

    lax.fori_loop(1, n, send_part, 0)

    for h in range(heads):
        for i in range(images):
            cols = slice(i * HEAD_SIZE, (i + 1) * HEAD_SIZE)
            kv_out[i, h] = jnp.concatenate([dk[h, :, cols], dv[h, :, cols]], axis=1).astype(BF16)

    term = dot(dq_send[mine], weight[...])
    for d in range(1, m):
        w_copy(d).wait_recv()
        dq_copy(d).wait_recv()
        term += dot(dq_recv[d], w_recv[d])
    text_out[...] = term.astype(BF16)

    at_mine = pl.ds(pl.multiple_of(lax.rem(me, bands) * band, 8), band)

    def reduce_band():
        sum_s[...] = part_s[at_mine]

        def add(d, c):
            part_copy(d).wait_recv()
            sum_s[...] += part_recv[d]
            return c

        lax.fori_loop(1, n, add, 0)

        def send_sum(d, c):
            sum_copy(d).start()
            return c

        lax.fori_loop(1, n, send_sum, 0)
        weight_out[at_mine] = sum_s[...]

    if_band(me, reduce_band)

    def place(d, c):
        frm = lax.rem(me + n - d, n)

        def put():
            sum_copy(d).wait_recv()
            weight_out[pl.ds(pl.multiple_of(frm * band, 8), band)] = sum_recv[d]

        if_band(frm, put)
        return c

    lax.fori_loop(1, n, place, 0)

    def drain(d, c):
        chunk_copy(d).wait_send()
        row_copy(d).wait_send()
        ret_copy(d).wait_send()
        if_band(lax.rem(me + d, n), lambda: part_copy(d).wait_send())
        if_band(me, lambda: sum_copy(d).wait_send())
        return c

    lax.fori_loop(1, n, drain, 0)

    def drain_mp(d, c):
        w_copy(d).wait_send()
        dq_copy(d).wait_send()
        return c

    lax.fori_loop(1, m, drain_mp, 0)


def per_device(texts, query_weight, patch_key_value, grad_out, negatives):
    n, m = lax.axis_size("dp"), lax.axis_size("mp")
    texts_here, length, _ = texts.shape
    images, heads, patches, _ = patch_key_value.shape
    captions = texts_here // images
    wanted = NEG * texts_here
    capacity = 2 * max(1, wanted // n)
    width, features = query_weight.shape
    tokens = texts_here * length
    count = -(-(capacity * length) // 16) * 16
    lanes = -(-count // 128) * 128
    share = -(-(tokens // m) // 16) * 16
    band = max(8, width // n)
    flat_text = texts.reshape(tokens, -1)
    grad_cols = lax.dynamic_slice_in_dim(grad_out, lax.axis_index("mp") * width, width, 3)
    grads = grad_cols.transpose(1, 0, 2, 3).reshape((NEG + 1) * tokens, width)

    flat_neg = negatives.reshape(-1)
    owner = flat_neg // images
    order = jnp.arange(wanted, dtype=jnp.int32)
    earlier = (owner[:, None] == owner[None, :]) & (order[None, :] < order[:, None])
    slot = owner * capacity + jnp.sum(earlier.astype(jnp.int32), axis=1)
    token = jnp.arange(lanes, dtype=jnp.int32)
    at = jnp.where(token < capacity * length, token // length, -n * capacity)
    place = jnp.arange(n, dtype=jnp.int32)[:, None] * capacity + at[None, :]
    found = place[:, :, None] == slot[None, None, :]
    text = order // NEG
    first = (order % NEG + 1) * tokens + text * length
    facts = jnp.stack([first, text * length, flat_neg % images], axis=0) + 1
    rows = jnp.sum(jnp.where(found[:, None], facts[None, :, None, :], 0), axis=3)
    inside = jnp.stack([token % length, token % length, jnp.zeros_like(token)], axis=0)
    rows = jnp.where(rows > 0, rows - 1 + inside[None], -1)
    rows = jnp.pad(rows, ((0, 0), (0, 5), (0, 0))).astype(F32)

    vmem = pl.BlockSpec(memory_space=pltpu.VMEM)
    box = (n, heads, count, 2 * HEAD_SIZE)
    wide = images * HEAD_SIZE
    dma = pltpu.SemaphoreType.DMA((n,))
    dma_mp = pltpu.SemaphoreType.DMA((m,))
    text_grad, weight_grad, key_value_grad = pl.pallas_call(
        functools.partial(kernel, n, m, heads, images, captions, length),
        out_shape=(
            jax.ShapeDtypeStruct((share, features), BF16),
            jax.ShapeDtypeStruct((width, features), F32),
            jax.ShapeDtypeStruct(patch_key_value.shape, BF16),
        ),
        in_specs=[vmem] * 5,
        out_specs=(vmem, vmem, vmem),
        scratch_shapes=[
            pltpu.VMEM((tokens, width), BF16),
            pltpu.VMEM((heads, tokens, 2 * HEAD_SIZE), BF16),
            pltpu.VMEM(box, BF16),
            pltpu.VMEM(box, BF16),
            pltpu.VMEM((n, 8, lanes), F32),
            pltpu.VMEM(box, BF16),
            pltpu.VMEM(box, BF16),
            pltpu.VMEM((heads, patches, wide), BF16),
            pltpu.VMEM((heads, patches, wide), BF16),
            pltpu.VMEM((heads, wide, patches), BF16),
            pltpu.VMEM((-(-patches // 128) * 128, wide), BF16),
            pltpu.VMEM((heads, patches, wide), F32),
            pltpu.VMEM((heads, patches, wide), F32),
            pltpu.VMEM((heads, tokens, 2 * HEAD_SIZE), F32),
            pltpu.VMEM((tokens, width), F32),
            pltpu.VMEM((m, share, width), BF16),
            pltpu.VMEM((m, share, width), BF16),
            pltpu.VMEM((m, width, features), BF16),
            pltpu.VMEM((width, features), F32),
            pltpu.VMEM((n, band, features), F32),
            pltpu.VMEM((band, features), F32),
            pltpu.VMEM((n, band, features), F32),
            dma, dma, dma, dma, dma, dma, dma, dma, dma, dma,
            dma_mp, dma_mp, dma_mp, dma_mp,
        ],
        compiler_params=pltpu.CompilerParams(
            collective_id=0, has_side_effects=True, vmem_limit_bytes=60 * 1024 * 1024
        ),
    )(flat_text, query_weight, grads, patch_key_value, rows)
    text_grad = text_grad[: tokens // m].reshape(texts_here // m, length, features)
    return (text_grad, weight_grad, key_value_grad)


def solution(mesh):
    in_specs = (
        P("dp", None, None),
        P("mp", None),
        P("dp", "mp", None, None),
        P("dp", None, None, None),
        P("dp", None),
    )
    out_specs = (P(("dp", "mp"), None, None), P("mp", None), P("dp", "mp", None, None))
    return jax.shard_map(
        per_device, mesh=mesh, in_specs=in_specs, out_specs=out_specs, check_vma=False
    )
```

time: 285 us -> 200 us (0.70)
  waiting for transfers between devices: 66.8 us -> 0 us
  Pallas kernels: 146 us -> 176 us
  local copies, waits for them, and re-layouts: 47.8 us -> 21.1 us
  between operations: 15.6 us -> 0.74 us
  matrix products: 5.02 us -> 0 us
    psum x1 -> x0, waiting for transfers between devices: 44.7 us -> none  [per_device(): weight_grad = lax.psum(weight_local, 'dp')]
    pallas_call x1, Pallas kernels: 146 us -> 176 us  [per_device(): pl.pallas_call(functools.partial(kernel, n, m, heads, images, captions, l...]
    reduce_scatter x1 -> x0, waiting for transfers between devices: 22.1 us -> none  [per_device(): lax.psum_scatter(text_term.reshape(texts_here, length, -1), 'mp', scatter...]
    transpose x3 -> x2, local copies, waits for them, and re-layouts: 12.5 us -> 2.15 us  [per_device(): grads = grad_cols.transpose(1, 0, 2, 3).reshape((NEG + 1) * tokens, width)]
    reshape x4 -> x2, local copies, waits for them, and re-layouts: 9.9 us -> 4.17 us  [the longest x1 2.47 us: per_device(): grads = grad_cols.transpose(1, 0, 2, 3).reshape((NEG + 1) * tokens, width)]
    broadcast_in_dim x9 -> x0, local copies, waits for them, and re-layouts: 5.36 us -> none  [the longest x1 1.83 us: per_device(): srcq[:, :, None]]
    slice x3 -> x0, local copies, waits for them, and re-layouts: 5.05 us -> none  [the longest x1 2.78 us: per_device(): g_own = grad_cols[:, 0].reshape(tokens, width)]
    dot_general x2 -> x0, matrix products: 5.02 us -> none  [dot(): return lax.dot_general(a, b, dims, preferred_element_type=F32)]
  transfers between devices with their start and end apart: 2 -> 0, of which waited for: 2 -> 0; matrix products, arithmetic and copies ran while one was open for 3% -> 0% of each run, Pallas kernels for 0% -> 0%
where the time goes in v2:
time: 200 us
  Pallas kernels  176 us (88%)
  local copies, waits for them, and re-layouts  21.1 us (11%)
    pallas_call x1, Pallas kernels, per_device(): pl.pallas_call(functools.partial(kernel, n, m, heads, images, captions, l...  176 us
    unnamed x10, local copies, waits for them, and re-layouts  12.2 us

profile of v2, /device:TPU:0, one launch (start us, length us, event | category | flops | bytes accessed | tf_op | source)
XLA Modules:
  0.0 199.6 jit_solution(6385443863731206179)
XLA Ops:
  0.6 0.0 copy-start
  0.7 0.9 copy.24
  1.7 0.1 reshape.314
  1.7 0.1 reshape.315
  1.9 0.2 convert_reduce_fusion
  2.1 0.1 broadcast_add_fusion
  2.2 0.2 broadcast_compare_fusion
  2.3 0.4 select_reduce_fusion
  2.7 0.7 pad_convert_fusion.rows
  3.4 2.4 %copy.22 = bf16[16,35,768]{2,1,0:T(8,128)(2,1)} copy(bf16[16,35,768]{2,0,1:T(8,128)(2,1)} %param.5) | data formatting | bytes 1720320 | tf_op args[0]
  5.8 2.4 %reshape.312.texts = bf16[560,768]{1,0:T(8,128)(2,1)} reshape(bf16[16,35,768]{2,1,0:T(8,128)(2,1)} %copy.22) | data formatting | bytes 1720320 | tf_op jit(solution)/shard_map/reshape | solution.py:312
  8.2 0.0 copy-done
  8.2 0.9 dynamic-slice_bitcast_fusion
  9.1 1.2 copy.23
  10.3 2.5 %reshape.313.grads = bf16[2240,192]{1,0:T(8,128)(2,1)} reshape(bf16[4,16,35,192]{3,2,1,0:T(8,128)(2,1)} %copy.23) | data formatting | bytes 1720320 | tf_op jit(solution)/shard_map/reshape | solution.py:314
  12.8 2.9 %copy.26.kv = bf16[4,3,577,128]{3,2,1,0:T(8,128)(2,1)} copy(bf16[4,3,577,128]{3,0,2,1:T(4,128)(2,1)} %param.7) | data formatting | bytes 3545088 | tf_op args[2]
  15.8 176.1 %shard_map.76 = (bf16[144,768]{1,0:T(8,128)(2,1)}, f32[192,768]{1,0:T(8,128)}, bf16[4,3,577,128]{3,2,1,0:T(8,128)(2,1)}) custom-call(bf16[560,768]{1,0:T(8,128)(2,1)} %reshape.312.texts, bf16[192,768]{1,0:T(8,128)(2,1)} %weight.1, bf16[2240,192]{1,0:T(8,128)(2,1)} %reshape.313.grads, bf16[4,3,577,128]{3,2,1,0:T(8,128)(2,1)} %copy.26.kv, ...), custom_call_target="tpu_custom_call" | custom-call | tf_op jit(solution)/shard_map/pallas_call | solution.py:338
  191.9 1.7 reshape.316
  193.6 1.7 copy.27
  195.3 0.0 copy-start.1
  195.3 3.4 %copy.28 = bf16[4,3,577,128]{3,0,2,1:T(4,128)(2,1)} copy(bf16[4,3,577,128]{3,2,1,0:T(8,128)(2,1)} %get-tuple-element.17) | data formatting | bytes 3545088
  198.7 0.0 copy-done.1
  198.7 0.8 copy.30
  (11 shorter events, 0.1 us)
Async XLA Ops:
  0.6 7.6 %copy-start = (bf16[16,4,35,768]{3,1,2,0:T(4,128)(2,1)S(1)}, bf16[16,4,35,768]{3,1,2,0:T(4,128)(2,1)}, u32[]{:S(2)}) copy-start(bf16[16,4,35,768]{3,1,2,0:T(4,128)(2,1)} %param.8) | copy-start | bytes 10321924
  195.3 3.4 %copy-start.1 = (f32[192,768]{1,0:T(8,128)S(1)}, f32[192,768]{1,0:T(8,128)}, u32[]{:S(2)}) copy-start(f32[192,768]{1,0:T(8,128)} %get-tuple-element.24) | copy-start | bytes 1769476

commit v3 on v2

--- a/solution.py
+++ b/solution.py
@@ -11,6 +11,7 @@
 NEG = 3
 F32 = jnp.float32
 BF16 = jnp.bfloat16
+LOG2E = 1.4426950408889634
 NN = (((1,), (0,)), ((), ()))
 NT = (((1,), (1,)), ((), ()))
 TN = (((0,), (0,)), ((), ()))
@@ -27,11 +28,11 @@
     gm = jnp.where(mask, jnp.concatenate([chunk[:, HEAD_SIZE:]] * images, axis=1), zero)
     scores = dot(km[h], qm, NT)
     top = jnp.max(scores, axis=0, keepdims=True)
-    e = jnp.exp((scores - top) * scale)
+    e = jnp.exp2((scores - top) * (scale * LOG2E))
     probs = e * (1.0 / jnp.sum(e, axis=0, keepdims=True))
     dprobs = dot(vm[h], gm, NT)
     center = jnp.sum(probs * dprobs, axis=0, keepdims=True)
-    ds = (probs * ((dprobs - center) * scale)).astype(BF16)
+    ds = (probs * (dprobs - center)).astype(BF16)
     dv[h] += dot(probs.astype(BF16), gm)
     dk[h] += dot(ds, qm)
     wide = dot(kmt[h], ds)
@@ -62,11 +63,21 @@
     bands = weight.shape[0] // band
     mesh_id = pl.DeviceIdType.MESH
 
+    def peer(j):
+        odd = lax.rem(j, 2)
+        k = odd * (n // 2) + j // 2
+        out = 0
+        bit = 1
+        while bit < n:
+            out = out + lax.rem(me // bit + k // bit, 2) * bit
+            bit *= 2
+        return out
+
     barrier = pltpu.get_barrier_semaphore()
 
     def greet_dp(d, c):
         pl.semaphore_signal(
-            barrier, inc=1, device_id={"dp": lax.rem(me + d, n)}, device_id_type=mesh_id
+            barrier, inc=1, device_id={"dp": peer(d)}, device_id_type=mesh_id
         )
         return c
 
@@ -90,22 +101,22 @@
         )
 
     def chunk_copy(d):
-        return dp_copy(send.at[d], recv.at[d], send_sem.at[d], recv_sem.at[d], lax.rem(me + d, n))
+        return dp_copy(send.at[d], recv.at[d], send_sem.at[d], recv_sem.at[d], peer(d))
 
     def row_copy(d):
-        to = lax.rem(me + d, n)
+        to = peer(d)
         return dp_copy(rows.at[to], rowrecv.at[d], id_send.at[d], id_recv.at[d], to)
 
     def ret_copy(d):
-        return dp_copy(ret.at[d], retrecv.at[d], ret_send.at[d], ret_recv.at[d], lax.rem(me + n - d, n))
+        return dp_copy(ret.at[d], retrecv.at[d], ret_send.at[d], ret_recv.at[d], peer(d))
 
     def part_copy(d):
-        to = lax.rem(me + d, n)
+        to = peer(d)
         at = pl.ds(pl.multiple_of(lax.rem(to, bands) * band, 8), band)
         return dp_copy(part_s.at[at], part_recv.at[d], part_ss.at[d], part_rs.at[d], to)
 
     def sum_copy(d):
-        return dp_copy(sum_s, sum_recv.at[d], sum_ss.at[d], sum_rs.at[d], lax.rem(me + d, n))
+        return dp_copy(sum_s, sum_recv.at[d], sum_ss.at[d], sum_rs.at[d], peer(d))
 
     def w_copy(d):
         return mp_copy(weight, w_recv.at[d], w_ss.at[d], w_rs.at[d], lax.rem(mine + d, m))
@@ -118,12 +129,12 @@
     pl.semaphore_wait(barrier, n + m - 2)
 
     def pack(d, c):
-        to = lax.rem(me + d, n)
+        to = peer(d)
         columns = rows[to].T[:count].astype(jnp.int32)
-        hot_g = (columns[:, 0:1] == lax.broadcasted_iota(jnp.int32, (count, total), 1)).astype(F32).astype(BF16)
+        hot_g = (columns[:, 0:1] == lax.broadcasted_iota(jnp.int32, (count, total - tokens), 1) + tokens).astype(F32).astype(BF16)
         hot_q = (columns[:, 1:2] == lax.broadcasted_iota(jnp.int32, (count, tokens), 1)).astype(F32).astype(BF16)
         pq = dot(hot_q, q_s[...]).astype(BF16)
-        pg = dot(hot_g, grads[...]).astype(BF16)
+        pg = dot(hot_g, grads[tokens:]).astype(BF16)
         for h in range(heads):
             cols = slice(h * HEAD_SIZE, (h + 1) * HEAD_SIZE)
             send[d, h] = jnp.concatenate([pq[:, cols], pg[:, cols]], axis=1)
@@ -143,7 +154,8 @@
     for h in range(heads):
         keys = jnp.concatenate([kv[i, h, :, :HEAD_SIZE] for i in range(images)], axis=1)
         km[h] = keys
-        vm[h] = jnp.concatenate([kv[i, h, :, HEAD_SIZE:] for i in range(images)], axis=1)
+        values = jnp.concatenate([kv[i, h, :, HEAD_SIZE:] for i in range(images)], axis=1)
+        vm[h] = values * jnp.asarray(HEAD_SIZE ** (-0.5), BF16)
         pad_s[:patches] = keys
         kmt[h] = pad_s[...].T[:, :patches]
     dk[...] = jnp.zeros_like(dk)
@@ -175,6 +187,19 @@
         == lax.broadcasted_iota(jnp.int32, (16, wide), 1) // HEAD_SIZE
     ).astype(F32).astype(BF16)
 
+    late = 3
+
+    def collect(d):
+        ret_copy(d).wait_recv()
+        row = rows[peer(d)][1:2, :count].astype(jnp.int32)
+        hot = (row == lax.broadcasted_iota(jnp.int32, (tokens, count), 0)).astype(F32).astype(BF16)
+
+        def head(h, c2):
+            dq_s[h] += dot(hot, retrecv[d, h])
+            return c2
+
+        lax.fori_loop(0, heads, head, 0)
+
     def serve(d, c):
         chunk_copy(d).wait_recv()
         row_copy(d).wait_recv()
@@ -191,23 +216,16 @@
 
         lax.fori_loop(0, heads, head, 0)
         ret_copy(d).start()
+
+        @pl.when(d > late)
+        def _():
+            collect(d - late)
+
         return c
 
     lax.fori_loop(1, n, serve, 0)
-
-    def collect(d, c):
-        ret_copy(d).wait_recv()
-        row = rows[lax.rem(me + d, n)][1:2, :count].astype(jnp.int32)
-        hot = (row == lax.broadcasted_iota(jnp.int32, (tokens, count), 0)).astype(F32).astype(BF16)
-
-        def head(h, c2):
-            dq_s[h] += dot(hot, retrecv[d, h])
-            return c2
-
-        lax.fori_loop(0, heads, head, 0)
-        return c
-
-    lax.fori_loop(1, n, collect, 0)
+    for d in range(max(1, n - late), n):
+        collect(d)
     parts = [dq_s[h, :, :HEAD_SIZE] + dq_s[h, :, HEAD_SIZE:] for h in range(heads)]
     dqf_s[...] = jnp.concatenate(parts, axis=1)
     dq_send[...] = jnp.zeros_like(dq_send)
@@ -228,7 +246,7 @@
             pl.when(who < bands)(f)
 
     def send_part(d, c):
-        if_band(lax.rem(me + d, n), lambda: part_copy(d).start())
+        if_band(peer(d), lambda: part_copy(d).start())
         return c
 
     lax.fori_loop(1, n, send_part, 0)
@@ -248,30 +266,29 @@
     at_mine = pl.ds(pl.multiple_of(lax.rem(me, bands) * band, 8), band)
 
     def reduce_band():
-        sum_s[...] = part_s[at_mine]
-
         def add(d, c):
             part_copy(d).wait_recv()
-            sum_s[...] += part_recv[d]
-            return c
-
-        lax.fori_loop(1, n, add, 0)
+            return c + part_recv[d]
+
+        band_sum = lax.fori_loop(1, n, add, part_s[at_mine])
+        padding = jnp.zeros((sum_s.shape[0] - band, band_sum.shape[1]), F32)
+        sum_s[...] = jnp.concatenate([band_sum, padding], axis=0).astype(BF16)
 
         def send_sum(d, c):
             sum_copy(d).start()
             return c
 
         lax.fori_loop(1, n, send_sum, 0)
-        weight_out[at_mine] = sum_s[...]
+        weight_out[at_mine] = sum_s[...].astype(F32)[:band]
 
     if_band(me, reduce_band)
 
     def place(d, c):
-        frm = lax.rem(me + n - d, n)
+        frm = peer(d)
 
         def put():
             sum_copy(d).wait_recv()
-            weight_out[pl.ds(pl.multiple_of(frm * band, 8), band)] = sum_recv[d]
+            weight_out[pl.ds(pl.multiple_of(frm * band, 8), band)] = sum_recv[d].astype(F32)[:band]
 
         if_band(frm, put)
         return c
@@ -282,7 +299,7 @@
         chunk_copy(d).wait_send()
         row_copy(d).wait_send()
         ret_copy(d).wait_send()
-        if_band(lax.rem(me + d, n), lambda: part_copy(d).wait_send())
+        if_band(peer(d), lambda: part_copy(d).wait_send())
         if_band(me, lambda: sum_copy(d).wait_send())
         return c
 
@@ -365,8 +382,8 @@
             pltpu.VMEM((m, width, features), BF16),
             pltpu.VMEM((width, features), F32),
             pltpu.VMEM((n, band, features), F32),
-            pltpu.VMEM((band, features), F32),
-            pltpu.VMEM((n, band, features), F32),
+            pltpu.VMEM((-(-band // 16) * 16, features), BF16),
+            pltpu.VMEM((n, -(-band // 16) * 16, features), BF16),
             dma, dma, dma, dma, dma, dma, dma, dma, dma, dma,
             dma_mp, dma_mp, dma_mp, dma_mp,
         ],

time: 200 us -> 178 us (0.89); the launches traced: 200 us -> 175 us
  Pallas kernels: 176 us -> 152 us
    pallas_call x1, Pallas kernels: 176 us -> 152 us  [per_device(): pl.pallas_call(functools.partial(kernel, n, m, heads, images, captions, l...]
where the time goes in v3:
time: 178 us; the launch traced here: 175 us
  Pallas kernels  152 us (85%)
  local copies, waits for them, and re-layouts  21.1 us (12%)
    pallas_call x1, Pallas kernels, per_device(): pl.pallas_call(functools.partial(kernel, n, m, heads, images, captions, l...  152 us
    unnamed x10, local copies, waits for them, and re-layouts  12.2 us

profile of v3, /device:TPU:0, one launch (start us, length us, event | category | flops | bytes accessed | tf_op | source)
XLA Modules:
  0.0 175.3 jit_solution(3200458862062892922)
XLA Ops:
  0.6 0.0 copy-start
  0.7 0.9 copy.24
  1.7 0.1 reshape.314
  1.7 0.1 reshape.315
  1.9 0.2 convert_reduce_fusion
  2.1 0.1 broadcast_add_fusion
  2.2 0.2 broadcast_compare_fusion
  2.3 0.4 select_reduce_fusion
  2.7 0.7 pad_convert_fusion.rows
  3.4 2.4 %copy.22 = bf16[16,35,768]{2,1,0:T(8,128)(2,1)} copy(bf16[16,35,768]{2,0,1:T(8,128)(2,1)} %param.5) | data formatting | bytes 1720320 | tf_op args[0]
  5.8 2.4 %reshape.312.texts = bf16[560,768]{1,0:T(8,128)(2,1)} reshape(bf16[16,35,768]{2,1,0:T(8,128)(2,1)} %copy.22) | data formatting | bytes 1720320 | tf_op jit(solution)/shard_map/reshape | solution.py:329
  8.2 0.0 copy-done
  8.2 0.9 dynamic-slice_bitcast_fusion
  9.1 1.2 copy.23
  10.3 2.5 %reshape.313.grads = bf16[2240,192]{1,0:T(8,128)(2,1)} reshape(bf16[4,16,35,192]{3,2,1,0:T(8,128)(2,1)} %copy.23) | data formatting | bytes 1720320 | tf_op jit(solution)/shard_map/reshape | solution.py:331
  12.8 2.9 %copy.26.kv = bf16[4,3,577,128]{3,2,1,0:T(8,128)(2,1)} copy(bf16[4,3,577,128]{3,0,2,1:T(4,128)(2,1)} %param.7) | data formatting | bytes 3545088 | tf_op args[2]
  15.8 151.9 %shard_map.76 = (bf16[144,768]{1,0:T(8,128)(2,1)}, f32[192,768]{1,0:T(8,128)}, bf16[4,3,577,128]{3,2,1,0:T(8,128)(2,1)}) custom-call(bf16[560,768]{1,0:T(8,128)(2,1)} %reshape.312.texts, bf16[192,768]{1,0:T(8,128)(2,1)} %weight.1, bf16[2240,192]{1,0:T(8,128)(2,1)} %reshape.313.grads, bf16[4,3,577,128]{3,2,1,0:T(8,128)(2,1)} %copy.26.kv, ...), custom_call_target="tpu_custom_call" | custom-call | tf_op jit(solution)/shard_map/pallas_call | solution.py:355
  167.7 1.7 reshape.316
  169.4 1.7 copy.27
  171.1 0.0 copy-start.1
  171.1 3.4 %copy.28 = bf16[4,3,577,128]{3,0,2,1:T(4,128)(2,1)} copy(bf16[4,3,577,128]{3,2,1,0:T(8,128)(2,1)} %get-tuple-element.17) | data formatting | bytes 3545088
  174.5 0.0 copy-done.1
  174.5 0.8 copy.30
  (11 shorter events, 0.1 us)
Async XLA Ops:
  0.6 7.6 %copy-start = (bf16[16,4,35,768]{3,1,2,0:T(4,128)(2,1)S(1)}, bf16[16,4,35,768]{3,1,2,0:T(4,128)(2,1)}, u32[]{:S(2)}) copy-start(bf16[16,4,35,768]{3,1,2,0:T(4,128)(2,1)} %param.8) | copy-start | bytes 10321924
  171.1 3.4 %copy-start.1 = (f32[192,768]{1,0:T(8,128)S(1)}, f32[192,768]{1,0:T(8,128)}, u32[]{:S(2)}) copy-start(f32[192,768]{1,0:T(8,128)} %get-tuple-element.24) | copy-start | bytes 1769476

commit v4 on v3

--- a/solution.py
+++ b/solution.py
@@ -46,7 +46,7 @@
     n, m, heads, images, captions, length,
     texts, weight, grads, kv, rows,
     text_out, weight_out, kv_out,
-    q_s, own_s, send, recv, rowrecv, ret, retrecv, km, vm, kmt, pad_s, dk, dv, dq_s, dqf_s,
+    q_s, own_s, send, recv, rowrecv, ret, retrecv, km, vm, kmt, pad_s, dk, dv, dq_s,
     dq_send, dq_recv, w_recv, part_s, part_recv, sum_s, sum_recv,
     send_sem, recv_sem, id_send, id_recv, ret_send, ret_recv, part_ss, part_rs, sum_ss, sum_rs,
     w_ss, w_rs, dq_ss, dq_rs,
@@ -165,13 +165,13 @@
         cols = slice(h * HEAD_SIZE, (h + 1) * HEAD_SIZE)
         own_s[h] = jnp.concatenate([qv[:, cols], gv[:, cols]], axis=1)
 
-    per_image = captions * length
+    held = captions * images
     own_mask = (
-        lax.broadcasted_iota(jnp.int32, (tokens, wide), 0) // per_image
+        lax.broadcasted_iota(jnp.int32, (tokens, wide), 0) % held // captions
         == lax.broadcasted_iota(jnp.int32, (tokens, wide), 1) // HEAD_SIZE
     )
     own_hot = (
-        lax.broadcasted_iota(jnp.int32, (16, tokens), 1) // per_image
+        lax.broadcasted_iota(jnp.int32, (16, tokens), 1) % held // captions
         == lax.broadcasted_iota(jnp.int32, (16, tokens), 0)
     ).astype(F32)
 
@@ -227,17 +227,21 @@
     for d in range(max(1, n - late), n):
         collect(d)
     parts = [dq_s[h, :, :HEAD_SIZE] + dq_s[h, :, HEAD_SIZE:] for h in range(heads)]
-    dqf_s[...] = jnp.concatenate(parts, axis=1)
-    dq_send[...] = jnp.zeros_like(dq_send)
+    dq = jnp.concatenate(parts, axis=1).astype(BF16)
+    some = held // m
+    row = lax.broadcasted_iota(jnp.int32, (share, tokens), 0)
+    row = jnp.where(row < piece, row // some * held + row % some, -held)
+    column = lax.broadcasted_iota(jnp.int32, (share, tokens), 1)
     for j in range(m):
-        dq_send[j, :piece] = dqf_s[j * piece : (j + 1) * piece].astype(BF16)
+        pick = (column == row + j * some).astype(F32).astype(BF16)
+        dq_send[j] = dot(pick, dq).astype(BF16)
 
     def send_dq(d, c):
         dq_copy(d).start()
         return c
 
     lax.fori_loop(1, m, send_dq, 0)
-    part_s[...] = dot(dqf_s[...].astype(BF16), texts[...], TN)
+    part_s[...] = dot(dq, texts[...], TN)
 
     def if_band(who, f):
         if bands == n:
@@ -326,9 +330,9 @@
     lanes = -(-count // 128) * 128
     share = -(-(tokens // m) // 16) * 16
     band = max(8, width // n)
-    flat_text = texts.reshape(tokens, -1)
+    flat_text = texts.transpose(1, 0, 2).reshape(tokens, -1)
     grad_cols = lax.dynamic_slice_in_dim(grad_out, lax.axis_index("mp") * width, width, 3)
-    grads = grad_cols.transpose(1, 0, 2, 3).reshape((NEG + 1) * tokens, width)
+    grads = grad_cols.transpose(1, 2, 0, 3).reshape((NEG + 1) * tokens, width)
 
     flat_neg = negatives.reshape(-1)
     owner = flat_neg // images
@@ -340,10 +344,11 @@
     place = jnp.arange(n, dtype=jnp.int32)[:, None] * capacity + at[None, :]
     found = place[:, :, None] == slot[None, None, :]
     text = order // NEG
-    first = (order % NEG + 1) * tokens + text * length
-    facts = jnp.stack([first, text * length, flat_neg % images], axis=0) + 1
+    first = (order % NEG + 1) * tokens + text
+    facts = jnp.stack([first, text, flat_neg % images], axis=0) + 1
     rows = jnp.sum(jnp.where(found[:, None], facts[None, :, None, :], 0), axis=3)
-    inside = jnp.stack([token % length, token % length, jnp.zeros_like(token)], axis=0)
+    step = token % length * texts_here
+    inside = jnp.stack([step, step, jnp.zeros_like(token)], axis=0)
     rows = jnp.where(rows > 0, rows - 1 + inside[None], -1)
     rows = jnp.pad(rows, ((0, 0), (0, 5), (0, 0))).astype(F32)
 
@@ -376,7 +381,6 @@
             pltpu.VMEM((heads, patches, wide), F32),
             pltpu.VMEM((heads, patches, wide), F32),
             pltpu.VMEM((heads, tokens, 2 * HEAD_SIZE), F32),
-            pltpu.VMEM((tokens, width), F32),
             pltpu.VMEM((m, share, width), BF16),
             pltpu.VMEM((m, share, width), BF16),
             pltpu.VMEM((m, width, features), BF16),
@@ -391,7 +395,7 @@
             collective_id=0, has_side_effects=True, vmem_limit_bytes=60 * 1024 * 1024
         ),
     )(flat_text, query_weight, grads, patch_key_value, rows)
-    text_grad = text_grad[: tokens // m].reshape(texts_here // m, length, features)
+    text_grad = text_grad[: tokens // m].reshape(length, texts_here // m, features).transpose(1, 0, 2)
     return (text_grad, weight_grad, key_value_grad)
 
 

time: 178 us -> 167 us (0.938)
  local copies, waits for them, and re-layouts: 21.1 us -> 10.6 us
    unnamed x10, local copies, waits for them, and re-layouts: 12.2 us -> 6.65 us
    reshape x3 -> x1, local copies, waits for them, and re-layouts: 6.58 us -> 1.68 us  [per_device(): text_grad[:tokens // m].reshape(length, texts_here // m, features)]
where the time goes in v4:
time: 167 us; the launch traced here: 165 us
  Pallas kernels  153 us (92%)
  local copies, waits for them, and re-layouts  10.6 us (6%)
    pallas_call x1, Pallas kernels, per_device(): pl.pallas_call(functools.partial(kernel, n, m, heads, images, captions, l...  153 us
    unnamed x10, local copies, waits for them, and re-layouts  6.65 us

profile of v4, /device:TPU:0, one launch (start us, length us, event | category | flops | bytes accessed | tf_op | source)
XLA Modules:
  0.0 165.5 jit_solution(4141811384192868747)
XLA Ops:
  0.6 0.0 copy-start
  0.7 0.9 copy.19
  1.7 0.1 reshape.314
  1.7 0.1 reshape.315
  1.9 0.2 convert_reduce_fusion
  2.1 0.1 broadcast_add_fusion
  2.2 0.2 broadcast_compare_fusion
  2.3 0.4 select_reduce_fusion
  2.7 0.7 pad_convert_fusion.rows
  3.4 0.0 copy-done
  3.4 0.0 copy-start.1
  3.4 0.9 dynamic-slice_bitcast_fusion
  4.3 1.2 copy.18
  5.5 0.0 copy-done.1
  5.5 1.5 copy.21.kv
  6.9 152.6 %shard_map.76 = (bf16[144,768]{1,0:T(8,128)(2,1)}, f32[192,768]{1,0:T(8,128)}, bf16[4,3,577,128]{3,2,1,0:T(8,128)(2,1)}) custom-call(bf16[560,768]{1,0:T(8,128)(2,1)} %bitcast.9, bf16[192,768]{1,0:T(8,128)(2,1)} %weight.1, bf16[2240,192]{1,0:T(8,128)(2,1)} %bitcast.8, bf16[4,3,577,128]{3,2,1,0:T(8,128)(2,1)} %copy.21.kv, f32[8,8,512]{2,1,0:T(8,128)} %pad_convert_fusion.rows), custom_call_target="tpu_custom_call" | custom-call | tf_op jit(solution)/shard_map/pallas_call | solution.py:360
  159.5 1.7 %reshape.316 = bf16[35,4,768]{2,1,0:T(4,128)(2,1)} reshape(bf16[140,768]{1,0:T(8,128)(2,1)} %bitcast.10) | data formatting | bytes 430080 | tf_op jit(solution)/shard_map/reshape | solution.py:398
  161.2 0.0 copy-start.2
  161.2 3.4 %copy.22 = bf16[4,3,577,128]{3,0,2,1:T(4,128)(2,1)} copy(bf16[4,3,577,128]{3,2,1,0:T(8,128)(2,1)} %get-tuple-element.17) | data formatting | bytes 3545088
  164.6 0.0 copy-done.2
  164.6 0.8 copy.24
  (11 shorter events, 0.1 us)
Async XLA Ops:
  0.6 2.8 %copy-start = (bf16[16,4,35,768]{3,1,2,0:T(4,128)(2,1)S(1)}, bf16[16,4,35,768]{3,1,2,0:T(4,128)(2,1)}, u32[]{:S(2)}) copy-start(bf16[16,4,35,768]{3,1,2,0:T(4,128)(2,1)} %param.8) | copy-start | bytes 10321924
  3.4 2.1 %copy-start.1 = (bf16[4,3,577,128]{3,0,2,1:T(4,128)(2,1)S(1)}, bf16[4,3,577,128]{3,0,2,1:T(4,128)(2,1)}, u32[]{:S(2)}) copy-start(bf16[4,3,577,128]{3,0,2,1:T(4,128)(2,1)} %param.7) | copy-start | bytes 5317636
  161.2 3.4 %copy-start.2 = (f32[192,768]{1,0:T(8,128)S(1)}, f32[192,768]{1,0:T(8,128)}, u32[]{:S(2)}) copy-start(f32[192,768]{1,0:T(8,128)} %get-tuple-element.24) | copy-start | bytes 1769476

commit v5 on v4

--- a/solution.py
+++ b/solution.py
@@ -46,14 +46,20 @@
     n, m, heads, images, captions, length,
     texts, weight, grads, kv, rows,
     text_out, weight_out, kv_out,
-    q_s, own_s, send, recv, rowrecv, ret, retrecv, km, vm, kmt, pad_s, dk, dv, dq_s,
+    q_s, q_all, own_s, chunk_s, send, recv, rowrecv, ret, retrecv, km, vm, kmt, pad_s, dk, dv, dq_s,
     dq_send, dq_recv, w_recv, part_s, part_recv, sum_s, sum_recv,
     send_sem, recv_sem, id_send, id_recv, ret_send, ret_recv, part_ss, part_rs, sum_ss, sum_rs,
-    w_ss, w_rs, dq_ss, dq_rs,
+    w_ss, w_rs, dq_ss, dq_rs, q_ys, q_zs, q_rs,
 ):
     me, mine = lax.axis_index("dp"), lax.axis_index("mp")
     tokens = texts.shape[0]
-    count = send.shape[2]
+    count = 2 * send.shape[1]
+    back = ret.shape[2]
+    width = weight.shape[0]
+    half = q_all.shape[1]
+    floors = n // 2
+    floor, side = me // 2, lax.rem(me, 2)
+    other = me + 1 - 2 * side
     total = grads.shape[0]
     wide = images * HEAD_SIZE
     patches = kv.shape[2]
@@ -125,19 +131,54 @@
         to = lax.rem(mine + d, m)
         return mp_copy(dq_send.at[to], dq_recv.at[d], dq_ss.at[d], dq_rs.at[d], to)
 
-    q_s[...] = dot(texts[...], weight[...], NT).astype(BF16)
+    def q_copy(src, to, ss):
+        return dp_copy(q_all.at[src], q_all.at[src], ss, q_rs.at[src], to)
+
+    def pass_on(hop):
+        @pl.when(floor - hop >= 0)
+        def _():
+            src = me - 2 * hop
+            q_copy(src, other, q_ys.at[src]).wait_recv()
+
+            @pl.when(floor + 1 < floors)
+            def _():
+                q_copy(src, me + 2, q_zs.at[src]).start()
+
+            q_copy(src, other, q_ys.at[src]).start()
+
+        @pl.when(floor + hop < floors)
+        def _():
+            src = me + 2 * hop
+            q_copy(src, other, q_ys.at[src]).wait_recv()
+
+            @pl.when(floor > 0)
+            def _():
+                q_copy(src, me - 2, q_zs.at[src]).start()
+
+            q_copy(src, other, q_ys.at[src]).start()
+
+    query = dot(texts[...], weight[...], NT).astype(BF16)
+    q_s[...] = query
+    low = jnp.concatenate([query[half:], jnp.zeros((2 * half - tokens, width), BF16)], axis=0)
+    q_all[me] = jnp.concatenate([query[:half], low], axis=1)
     pl.semaphore_wait(barrier, n + m - 2)
+
+    @pl.when(floor + 1 < floors)
+    def _():
+        q_copy(me, me + 2, q_zs.at[me]).start()
+
+    @pl.when(floor > 0)
+    def _():
+        q_copy(me, me - 2, q_zs.at[n]).start()
+
+    q_copy(me, other, q_ys.at[me]).start()
 
     def pack(d, c):
         to = peer(d)
         columns = rows[to].T[:count].astype(jnp.int32)
         hot_g = (columns[:, 0:1] == lax.broadcasted_iota(jnp.int32, (count, total - tokens), 1) + tokens).astype(F32).astype(BF16)
-        hot_q = (columns[:, 1:2] == lax.broadcasted_iota(jnp.int32, (count, tokens), 1)).astype(F32).astype(BF16)
-        pq = dot(hot_q, q_s[...]).astype(BF16)
         pg = dot(hot_g, grads[tokens:]).astype(BF16)
-        for h in range(heads):
-            cols = slice(h * HEAD_SIZE, (h + 1) * HEAD_SIZE)
-            send[d, h] = jnp.concatenate([pq[:, cols], pg[:, cols]], axis=1)
+        send[d] = jnp.concatenate([pg[: count // 2], pg[count // 2 :]], axis=1)
         chunk_copy(d).start()
         row_copy(d).start()
         return c
@@ -178,9 +219,21 @@
     def own_head(h, c):
         dq = attend(h, own_s[h], own_mask, own_hot, km, vm, kmt, dk, dv, images)
         dq_s[h] = jnp.concatenate([dq, jnp.zeros_like(dq)], axis=1)
+
+        @pl.when(h + 1 < floors)
+        def _():
+            pass_on(h + 1)
+
         return c
 
     lax.fori_loop(0, heads, own_head, 0)
+
+    def more(hop, c):
+        pass_on(hop)
+        return c
+
+    if floors > heads + 1:
+        lax.fori_loop(heads + 1, floors, more, 0)
 
     spread = (
         lax.broadcasted_iota(jnp.int32, (16, wide), 0)
@@ -191,8 +244,8 @@
 
     def collect(d):
         ret_copy(d).wait_recv()
-        row = rows[peer(d)][1:2, :count].astype(jnp.int32)
-        hot = (row == lax.broadcasted_iota(jnp.int32, (tokens, count), 0)).astype(F32).astype(BF16)
+        row = rows[peer(d)][1:2, :back].astype(jnp.int32)
+        hot = (row == lax.broadcasted_iota(jnp.int32, (tokens, back), 0)).astype(F32).astype(BF16)
 
         def head(h, c2):
             dq_s[h] += dot(hot, retrecv[d, h])
@@ -206,9 +259,25 @@
         named = rowrecv[d][2:3, :count].astype(jnp.int32)
         hot = (named == lax.broadcasted_iota(jnp.int32, (16, count), 0)).astype(F32)
         mask = dot(hot.astype(BF16), spread, TN) > 0.5
+        frm = peer(d)
+
+        @pl.when(lax.rem(frm, 2) != side)
+        def _():
+            q_copy(frm, other, q_ys.at[frm]).wait_recv()
+
+        column = rowrecv[d].T[:count, 1:2].astype(jnp.int32)
+        lane = lax.broadcasted_iota(jnp.int32, (count, half), 1)
+        pq = dot((column == lane).astype(F32).astype(BF16), q_all[frm, :, :width])
+        pq += dot((column == lane + half).astype(F32).astype(BF16), q_all[frm, :, width:])
+        pq = pq.astype(BF16)
+        pg = jnp.concatenate([recv[d, :, :width], recv[d, :, width:]], axis=0)
+        for h in range(heads):
+            cols = slice(h * HEAD_SIZE, (h + 1) * HEAD_SIZE)
+            chunk_s[h] = jnp.concatenate([pq[:, cols], pg[:, cols]], axis=1)
 
         def head(h, c2):
-            dq = attend(h, recv[d, h], mask, hot, km, vm, kmt, dk, dv, images)
+            dq = attend(h, chunk_s[h], mask, hot, km, vm, kmt, dk, dv, images)
+            dq = dq[:back]
             hi = dq.astype(BF16)
             lo = (dq - hi.astype(F32)).astype(BF16)
             ret[d, h] = jnp.concatenate([hi, lo], axis=1)
@@ -309,6 +378,26 @@
 
     lax.fori_loop(1, n, drain, 0)
 
+    def drain_q(z, c):
+        src = 2 * z + side
+        q_copy(src, other, q_ys.at[src]).wait_send()
+
+        @pl.when((z <= floor) & (floor + 1 < floors))
+        def _():
+            q_copy(src, other, q_zs.at[src]).wait_send()
+
+        @pl.when((z > floor) & (floor > 0))
+        def _():
+            q_copy(src, other, q_zs.at[src]).wait_send()
+
+        return c
+
+    lax.fori_loop(0, floors, drain_q, 0)
+
+    @pl.when(floor > 0)
+    def _():
+        q_copy(me, other, q_zs.at[n]).wait_send()
+
     def drain_mp(d, c):
         w_copy(d).wait_send()
         dq_copy(d).wait_send()
@@ -326,7 +415,9 @@
     capacity = 2 * max(1, wanted // n)
     width, features = query_weight.shape
     tokens = texts_here * length
-    count = -(-(capacity * length) // 16) * 16
+    count = -(-(capacity * length) // 32) * 32
+    back = -(-(capacity * length) // 16) * 16
+    half = -(-tokens // 32) * 16
     lanes = -(-count // 128) * 128
     share = -(-(tokens // m) // 16) * 16
     band = max(8, width // n)
@@ -353,7 +444,8 @@
     rows = jnp.pad(rows, ((0, 0), (0, 5), (0, 0))).astype(F32)
 
     vmem = pl.BlockSpec(memory_space=pltpu.VMEM)
-    box = (n, heads, count, 2 * HEAD_SIZE)
+    box = (n, heads, back, 2 * HEAD_SIZE)
+    grad_box = (n, count // 2, 2 * width)
     wide = images * HEAD_SIZE
     dma = pltpu.SemaphoreType.DMA((n,))
     dma_mp = pltpu.SemaphoreType.DMA((m,))
@@ -368,9 +460,11 @@
         out_specs=(vmem, vmem, vmem),
         scratch_shapes=[
             pltpu.VMEM((tokens, width), BF16),
+            pltpu.VMEM((n, half, 2 * width), BF16),
             pltpu.VMEM((heads, tokens, 2 * HEAD_SIZE), BF16),
-            pltpu.VMEM(box, BF16),
-            pltpu.VMEM(box, BF16),
+            pltpu.VMEM((heads, count, 2 * HEAD_SIZE), BF16),
+            pltpu.VMEM(grad_box, BF16),
+            pltpu.VMEM(grad_box, BF16),
             pltpu.VMEM((n, 8, lanes), F32),
             pltpu.VMEM(box, BF16),
             pltpu.VMEM(box, BF16),
@@ -390,6 +484,7 @@
             pltpu.VMEM((n, -(-band // 16) * 16, features), BF16),
             dma, dma, dma, dma, dma, dma, dma, dma, dma, dma,
             dma_mp, dma_mp, dma_mp, dma_mp,
+            dma, pltpu.SemaphoreType.DMA((n + 1,)), dma,
         ],
         compiler_params=pltpu.CompilerParams(
             collective_id=0, has_side_effects=True, vmem_limit_bytes=60 * 1024 * 1024

time: 167 us -> 159 us (0.952)
  Pallas kernels: 153 us -> 144 us
    pallas_call x1, Pallas kernels: 153 us -> 144 us  [per_device(): pl.pallas_call(functools.partial(kernel, n, m, heads, images, captions, l...]
where the time goes in v5:
time: 159 us; the launch traced here: 157 us
  Pallas kernels  144 us (91%)
  local copies, waits for them, and re-layouts  10.6 us (7%)
  other arithmetic  1.59 us (1%)
    pallas_call x1, Pallas kernels, per_device(): pl.pallas_call(functools.partial(kernel, n, m, heads, images, captions, l...  144 us
    unnamed x10, local copies, waits for them, and re-layouts  6.65 us

profile of v5, /device:TPU:0, one launch (start us, length us, event | category | flops | bytes accessed | tf_op | source)
XLA Modules:
  0.0 157.0 jit_solution(4457935568004706376)
XLA Ops:
  0.6 0.0 copy-start
  0.7 0.9 copy.19
  1.7 0.1 reshape.314
  1.7 0.1 reshape.315
  1.9 0.2 convert_reduce_fusion
  2.1 0.1 broadcast_add_fusion
  2.2 0.2 broadcast_compare_fusion
  2.3 0.4 select_reduce_fusion
  2.7 0.7 pad_convert_fusion.rows
  3.4 0.0 copy-done
  3.4 0.0 copy-start.1
  3.4 0.9 dynamic-slice_bitcast_fusion
  4.3 1.2 copy.18
  5.5 0.0 copy-done.1
  5.5 1.5 copy.21.kv
  6.9 144.1 %shard_map.76 = (bf16[144,768]{1,0:T(8,128)(2,1)}, f32[192,768]{1,0:T(8,128)}, bf16[4,3,577,128]{3,2,1,0:T(8,128)(2,1)}) custom-call(bf16[560,768]{1,0:T(8,128)(2,1)} %bitcast.9, bf16[192,768]{1,0:T(8,128)(2,1)} %weight.1, bf16[2240,192]{1,0:T(8,128)(2,1)} %bitcast.8, bf16[4,3,577,128]{3,2,1,0:T(8,128)(2,1)} %copy.21.kv, f32[8,8,512]{2,1,0:T(8,128)} %pad_convert_fusion.rows), custom_call_target="tpu_custom_call" | custom-call | tf_op jit(solution)/shard_map/pallas_call | solution.py:452
  151.1 1.7 %reshape.316 = bf16[35,4,768]{2,1,0:T(4,128)(2,1)} reshape(bf16[140,768]{1,0:T(8,128)(2,1)} %bitcast.10) | data formatting | bytes 430080 | tf_op jit(solution)/shard_map/reshape | solution.py:493
  152.8 0.0 copy-start.2
  152.8 3.4 %copy.22 = bf16[4,3,577,128]{3,0,2,1:T(4,128)(2,1)} copy(bf16[4,3,577,128]{3,2,1,0:T(8,128)(2,1)} %get-tuple-element.17) | data formatting | bytes 3545088
  156.2 0.0 copy-done.2
  156.2 0.8 copy.24
  (11 shorter events, 0.1 us)
Async XLA Ops:
  0.6 2.8 %copy-start = (bf16[16,4,35,768]{3,1,2,0:T(4,128)(2,1)S(1)}, bf16[16,4,35,768]{3,1,2,0:T(4,128)(2,1)}, u32[]{:S(2)}) copy-start(bf16[16,4,35,768]{3,1,2,0:T(4,128)(2,1)} %param.8) | copy-start | bytes 10321924
  3.4 2.1 %copy-start.1 = (bf16[4,3,577,128]{3,0,2,1:T(4,128)(2,1)S(1)}, bf16[4,3,577,128]{3,0,2,1:T(4,128)(2,1)}, u32[]{:S(2)}) copy-start(bf16[4,3,577,128]{3,0,2,1:T(4,128)(2,1)} %param.7) | copy-start | bytes 5317636
  152.8 3.4 %copy-start.2 = (f32[192,768]{1,0:T(8,128)S(1)}, f32[192,768]{1,0:T(8,128)}, u32[]{:S(2)}) copy-start(f32[192,768]{1,0:T(8,128)} %get-tuple-element.24) | copy-start | bytes 1769476
